TPU v7x, 256 devices: a whole 4x4x8 slice. The times are simulated.
256 devices in a mesh: stream: 4 (over x_lo, core), span: 64 (over z, y, x_hi).
Axes of the slice: x: 4 (x_hi: 2, x_lo: 2; x = x_hi * 2 + x_lo), y: 4, z: 8, core: 2. Of those that a mesh axis runs over, the one named last changes fastest.
Arguments:
- species: float32 [9, 32, 1024, 128], P(None, 'stream', 'span'), may hold values from 0 to 1
- flow: float32 [5, 32, 1024, 128], P(None, 'stream', 'span'), may hold values from -3 to 3
- interp_index: int32 [2, 128], replicated, may hold values from 0 to 126
- interp_frac: float32 [2, 128], replicated, may hold values from 0 to 1
- mean_gain: float32 [2, 14], replicated, may hold values from 1.5 to 4
- fluct_gain: float32 [2, 14], replicated, may hold values from 0.3 to 1
- reaction_table: int32 [21, 3], replicated, may hold values from 0 to 8
- rate_const: float32 [21], replicated, may hold values from 0.3 to 3
- activation: float32 [21], replicated, may hold values from 0.5 to 2
- heat_release: float32 [21], replicated, may hold values from 0.2 to 1
Outputs:
- species_next: float32 [9, 32, 1024, 128], P(None, 'stream', 'span')
- flow_next: float32 [5, 32, 1024, 128], P(None, 'stream', 'span')
Inputs may be any that keep to these rules, and one draw needn't show every extreme that they name: `reaction_table`: a reactant may appear twice.
All inputs are finite; a program needn't handle non-finite values.
Results may differ from a plain program's by a relative error of at most 0.0003.
Values sent between devices are 32-bit elements; how exact they have to be, the bound alone decides.
A program may use at most 128 MiB of HBM per device.

v0:
```python
import jax
import jax.numpy as jnp
from jax import lax
from jax.sharding import PartitionSpec as P

STENCIL = (0.8, -0.2, 4.0 / 105.0, -1.0 / 280.0)
TIMESTEP = 0.2
VISCOSITY = 0.1


def from_behind(array, axis, by):
    length = lax.axis_size(axis)
    pairs = [(i, i + by) for i in range(length) if 0 <= i + by < length]
    return lax.ppermute(array, axis, pairs)


def from_behind_2(value, axis, steps):
    count = lax.axis_size(axis)
    pairs = [(source, (source + steps) % count) for source in range(count)]
    return lax.ppermute(value, axis, pairs)


def padded_2(block, sides, width):
    for axis, dim in sides:
        count = lax.axis_size(axis)
        forward = [(i, i + 1) for i in range(count - 1)]
        forward.append((count - 1, 0))
        backward = [(target, source) for source, target in forward]
        low = lax.ppermute(
            lax.slice_in_dim(block, block.shape[dim] - width, None, axis=dim), axis, forward
        )
        high = lax.ppermute(lax.slice_in_dim(block, 0, width, axis=dim), axis, backward)
        block = jnp.concatenate([low, block, high], axis=dim)
    return block


def interpolate(values, index_row, frac_row):
    lower = jnp.take(values, index_row, axis=-1)
    upper = jnp.take(values, index_row + 1, axis=-1)
    return (1.0 - frac_row) * lower + frac_row * upper


def rescale(slab, mean, interp_index, interp_frac, mean_gain, fluct_gain):
    fluct = slab - mean[:, :, None, :]
    height = slab.shape[-1]
    levels = jnp.arange(height).astype(jnp.float32) / (height - 1.0)
    blend = 0.5 * (1.0 + jnp.tanh(6.0 * (levels - 0.5)))
    parts = []
    for branch in range(2):
        mean_part = interpolate(mean, interp_index[branch], interp_frac[branch])
        fluct_part = interpolate(fluct, interp_index[branch], interp_frac[branch])
        parts.append(
            mean_gain[branch][:, None, None, None] * mean_part[:, :, None, :]
            + fluct_gain[branch][:, None, None, None] * fluct_part
        )
    return (1.0 - blend) * parts[0] + blend * parts[1]


def difference(padded, axis, count):
    total = jnp.zeros_like(lax.slice_in_dim(padded, 4, 4 + count, axis=axis))
    for offset in range(1, 5):
        ahead = lax.slice_in_dim(padded, 4 + offset, 4 + offset + count, axis=axis)
        behind = lax.slice_in_dim(padded, 4 - offset, 4 - offset + count, axis=axis)
        total = total + STENCIL[offset - 1] * (ahead - behind)
    return total


def tendency(across, ghost, reaction_table, rate_const, activation, heat_release):
    state = across[:, :, 4:-4]
    width = state.shape[2]
    following = from_behind(state[:, :4], "stream", -1)
    group = lax.axis_index("stream")
    groups = lax.axis_size("stream")
    tail = jnp.where(group == groups - 1, jnp.repeat(state[:, -1:], 4, axis=1), following)
    along = jnp.concatenate([ghost, state, tail], 1)
    slope_x = difference(along, 1, state.shape[1])
    slope_z = difference(across, 2, width)
    advection = (1.0 + state[9]) * slope_x + state[11] * slope_z
    floor_pad = jnp.zeros_like(state[..., :1])
    vertical = jnp.concatenate([floor_pad, state, state[..., -1:]], -1)
    curvature = vertical[..., 2:] - 2.0 * state + vertical[..., :-2]
    cold = jnp.exp(-state[13])
    nspecies = 9
    first = jnp.take(state, reaction_table[:, 0], axis=0)
    second = jnp.take(state, reaction_table[:, 1], axis=0)
    rates = (
        rate_const[:, None, None, None]
        * jnp.exp(-activation[:, None, None, None] * cold[None])
        * first
        * second
    )
    labels = jnp.arange(nspecies)[None, :]
    weight = (
        2.0 * (reaction_table[:, 2:3] == labels).astype(jnp.float32)
        - (reaction_table[:, 0:1] == labels).astype(jnp.float32)
        - (reaction_table[:, 1:2] == labels).astype(jnp.float32)
    )
    spec_source = jnp.einsum("rs,rxzy->sxzy", weight, rates, precision=lax.Precision.HIGHEST)
    heat_source = jnp.einsum("r,rxzy->xzy", heat_release, rates, precision=lax.Precision.HIGHEST)
    middle_zero = jnp.zeros_like(state[nspecies:13])
    source = jnp.concatenate([spec_source, middle_zero, heat_source[None]], 0)
    return -advection + VISCOSITY * curvature + source


def recycle(source, core_lo, core_hi, interp_index, interp_frac, mean_gain, fluct_gain):
    depth = source.shape[1]
    slab = source[:, depth - 4 : depth]
    total_z = (core_hi - core_lo) * lax.axis_size("span")
    sums = jnp.sum(slab, 2)
    mean = lax.psum(sums, "span") / total_z
    arrived, arrived_mean = from_behind_2((slab, mean), "stream", 1)
    return rescale(arrived, arrived_mean, interp_index, interp_frac, mean_gain, fluct_gain)


def on_device(
    species,
    flow,
    interp_index,
    interp_frac,
    mean_gain,
    fluct_gain,
    reaction_table,
    rate_const,
    activation,
    heat_release,
):
    start = jnp.concatenate([species, flow], 0)
    slab_width = species.shape[2]
    nspecies = species.shape[0]
    extra = (reaction_table, rate_const, activation, heat_release)
    rescaling = (interp_index, interp_frac, mean_gain, fluct_gain)
    ghost = recycle(start, 0, slab_width, *rescaling)

    def spread(state):
        return padded_2(state, (("span", 2),), 4)

    lifted = start + TIMESTEP * tendency(spread(start), ghost, *extra)
    middle = 0.75 * start + 0.25 * (lifted + TIMESTEP * tendency(spread(lifted), ghost, *extra))
    final = start / 3.0 + 2.0 / 3.0 * (middle + TIMESTEP * tendency(spread(middle), ghost, *extra))
    return (final[:nspecies], final[nspecies:])


def solution(mesh):
    return jax.shard_map(
        on_device,
        mesh=mesh,
        in_specs=(
            P(None, "stream", "span", None),
            P(None, "stream", "span", None),
            P(),
            P(),
            P(),
            P(),
            P(),
            P(),
            P(),
            P(),
        ),
        out_specs=(P(None, "stream", "span", None), P(None, "stream", "span", None)),
        check_vma=False,
    )
```

profile of v0, /device:TPU:6, one launch (start us, length us, event | category | flops | bytes accessed | tf_op | source)
XLA Modules:
  0.0 511.0 jit_solution(12147093496554436039)
XLA Ops:
  3.1 354.3 %psum.7 = f32[14,4,128]{0,1,2:T(4,128)S(1)} all-reduce(f32[14,4,128]{0,1,2:T(4,128)S(1)} %copy.69), channel_id=1, replica_groups=mesh['stream'=4,'span'=64] {'span'}, use_global_device_ids=true, to_apply=%region_1.0 | all-reduce | flops 7168 | bytes 57344 | tf_op jit(solution)/shard_map/psum | solution.py:110
  359.1 2.7 collective-permute-start
  362.7 8.2 %collective-permute-start.3 = (f32[14,8,4,128]{3,2,1,0:T(4,128)}, f32[14,8,4,128]{3,2,1,0:T(4,128)}, u32[]{:S(2)}, u32[]{:S(2)}) collective-permute-start(f32[14,8,4,128]{3,2,1,0:T(4,128)} %get-tuple-element.33), channel_id=1, source_target_pairs={{1,0},{2,1},{3,2},{4,3},{5,4},{6,5},{7,6},{8,7},{9,8},{10,9},{11,1... | collective-permute-start | bytes 688136 | tf_op jit(solution)/shard_map/ppermute | solution.py:32
  379.4 1.8 select_multiply_fusion.4
  381.2 1.9 fusion.8
  392.8 3.4 copy.73
  396.2 7.2 %gather_fusion.2 = f32[128,14,4,16]{3,2,1,0:T(4,128)} fusion(f32[14,4,16,128]{2,1,3,0:T(4,128)} %copy.73, s32[1024]{0:T(1024)} %pad_clamp_fusion.5), kind=kCustom, calls=%fused_computation.1.clone | custom fusion | bytes 918016 | tf_op jit(solution)/shard_map/jit(_take)/gather | solution.py:38
  403.4 7.2 %gather_fusion.3 = f32[128,14,4,16]{3,2,1,0:T(4,128)} fusion(f32[14,4,16,128]{2,1,3,0:T(4,128)} %copy.73, s32[1024]{0:T(1024)} %pad_clamp_fusion.4), kind=kCustom, calls=%fused_computation.6.clone | custom fusion | bytes 918016 | tf_op jit(solution)/shard_map/jit(_take)/gather | solution.py:39
  410.6 7.1 %gather_fusion.6 = f32[128,14,4,16]{3,2,1,0:T(4,128)} fusion(f32[14,4,16,128]{2,1,3,0:T(4,128)} %copy.73, s32[1024]{0:T(1024)S(1)} %pad_clamp_fusion.3), kind=kCustom, calls=%fused_computation.7.clone | custom fusion | bytes 918016 | tf_op jit(solution)/shard_map/jit(_take)/gather | solution.py:38
  417.6 7.0 %gather_fusion.7 = f32[128,14,4,16]{3,2,1,0:T(4,128)} fusion(f32[14,4,16,128]{2,1,3,0:T(4,128)} %copy.73, s32[1024]{0:T(1024)S(1)} %pad_clamp_fusion.2), kind=kCustom, calls=%fused_computation.8.clone | custom fusion | bytes 918016 | tf_op jit(solution)/shard_map/jit(_take)/gather | solution.py:39
  424.7 3.5 copy.74
  428.2 3.5 copy.76
  431.7 4.1 copy.80
  435.9 4.2 copy.82
  442.9 4.1 fusion.21
  447.1 1.9 gather_fusion.10
  448.9 1.9 gather_fusion.11
  453.1 1.8 fusion.6
  455.2 1.9 collective-permute-start.5
  457.1 3.6 collective-permute-start.6
  461.6 1.9 fusion.4
  464.8 4.9 collective-permute-done.6
  469.7 3.2 collective-permute-done.7
  472.9 2.7 fusion.33
  475.6 1.9 gather_fusion.12
  477.5 1.9 gather_fusion.13
  483.7 1.9 collective-permute-start.8
  485.6 5.0 collective-permute-start.10
  491.3 1.9 fusion
  493.2 9.2 %collective-permute-done.10 = f32[14,8,4,128]{3,2,1,0:T(4,128)S(1)} collective-permute-done((f32[14,8,4,128]{3,2,1,0:T(4,128)S(1)}, f32[14,8,4,128]{3,2,1,0:T(4,128)S(1)}, u32[]{:S(2)}, u32[]{:S(2)}) %collective-permute-start.10) | collective-permute-done | bytes 229408 | tf_op jit(solution)/shard_map/ppermute | solution.py:29
  502.4 4.3 collective-permute-done.9
  506.7 2.5 fusion.45
  (171 shorter events, 36.8 us)
Async XLA Ops:
  0.6 380.6 %copy-start = (f32[21]{0:T(128)S(1)}, f32[21]{0:T(128)}, u32[]{:S(2)}) copy-start(f32[21]{0:T(128)} %param.25) | copy-start | bytes 256
  2.9 368.0 %copy-start.37 = (f32[2,128]{1,0:T(2,128)S(1)}, f32[2,128]{1,0:T(2,128)}, u32[]{:S(2)}) copy-start(f32[2,128]{1,0:T(2,128)} %param.19) | copy-start | bytes 3076
  2.9 369.9 %copy-start.38 = (s32[21,3]{0,1:T(4,128)S(1)}, s32[21,3]{0,1:T(4,128)}, u32[]{:S(2)}) copy-start(s32[21,3]{0,1:T(4,128)} %param.22) | copy-start | bytes 760
  2.9 370.6 %copy-start.43 = (s32[2,128]{1,0:T(2,128)S(1)}, s32[2,128]{1,0:T(2,128)}, u32[]{:S(2)}) copy-start(s32[2,128]{1,0:T(2,128)} %param.18) | copy-start | bytes 3076
  3.1 372.1 %copy-start.44 = (f32[2,14]{1,0:T(2,128)S(1)}, f32[2,14]{1,0:T(2,128)}, u32[]{:S(2)}) copy-start(f32[2,14]{1,0:T(2,128)} %param.20) | copy-start | bytes 340
  3.1 372.7 %copy-start.45 = (f32[2,14]{1,0:T(2,128)S(1)}, f32[2,14]{1,0:T(2,128)}, u32[]{:S(2)}) copy-start(f32[2,14]{1,0:T(2,128)} %param.21) | copy-start | bytes 340
  358.1 29.4 %collective-permute-start.1 = (f32[14,4,128]{0,1,2:T(4,128)}, f32[14,4,128]{0,1,2:T(4,128)S(1)}, u32[]{:S(2)}, u32[]{:S(2)}) collective-permute-start(f32[14,4,128]{0,1,2:T(4,128)} %broadcast_multiply_fusion), channel_id=1, source_target_pairs={{0,64},{64,128},{128,192},{192,0},{1,65},{65,129},{129,193},{193,1... | collective-permute-start | bytes 86024 | tf_op jit(solution)/shard_map/ppermute | solution.py:20
  358.1 33.6 %collective-permute-start.2 = (f32[14,4,16,128]{3,2,1,0:T(8,128)}, f32[14,4,16,128]{3,2,1,0:T(8,128)}, u32[]{:S(2)}, u32[]{:S(2)}) collective-permute-start(f32[14,4,16,128]{3,2,1,0:T(8,128)} %get-tuple-element.37), channel_id=1, source_target_pairs={{0,64},{64,128},{128,192},{192,0},{1,65},{65,129},{129,193},{193,1... | collective-permute-start | bytes 1376264 | tf_op jit(solution)/shard_map/ppermute | solution.py:20
  359.1 82.7 %collective-permute-start = (f32[14,4,16,128]{3,2,1,0:T(8,128)}, f32[14,4,16,128]{3,2,1,0:T(8,128)}, u32[]{:S(2)}, u32[]{:S(2)}) collective-permute-start(f32[14,4,16,128]{3,2,1,0:T(8,128)} %get-tuple-element.35), channel_id=1, source_target_pairs={{64,0},{128,64},{192,128},{65,1},{129,65},{193,129},{66,2},{130,66... | collective-permute-start | bytes 1376264 | tf_op jit(solution)/shard_map/ppermute | solution.py:14
  362.7 80.1 %collective-permute-start.3 = (f32[14,8,4,128]{3,2,1,0:T(4,128)}, f32[14,8,4,128]{3,2,1,0:T(4,128)}, u32[]{:S(2)}, u32[]{:S(2)}) collective-permute-start(f32[14,8,4,128]{3,2,1,0:T(4,128)} %get-tuple-element.33), channel_id=1, source_target_pairs={{1,0},{2,1},{3,2},{4,3},{5,4},{6,5},{7,6},{8,7},{9,8},{10,9},{11,1... | collective-permute-start | bytes 688136 | tf_op jit(solution)/shard_map/ppermute | solution.py:32
  370.9 72.0 %collective-permute-start.4 = (f32[14,8,4,128]{3,2,1,0:T(4,128)}, f32[14,8,4,128]{3,2,1,0:T(4,128)}, u32[]{:S(2)}, u32[]{:S(2)}) collective-permute-start(f32[14,8,4,128]{3,2,1,0:T(4,128)} %get-tuple-element.34), channel_id=1, source_target_pairs={{0,1},{1,2},{2,3},{3,4},{4,5},{5,6},{6,7},{7,8},{8,9},{9,10},{10,1... | collective-permute-start | bytes 688136 | tf_op jit(solution)/shard_map/ppermute | solution.py:29
  372.8 6.1 %copy-start.10 = (pred[21]{0:T(512)(128)(4,1)}, pred[21]{0:T(512)(128)(4,1)S(1)}, u32[]{:S(2)}) copy-start(pred[21]{0:T(512)(128)(4,1)S(1)} %get-tuple-element.11) | copy-start | bytes 67
  372.8 6.1 %copy-start.12 = (pred[21]{0:T(512)(128)(4,1)}, pred[21]{0:T(512)(128)(4,1)S(1)}, u32[]{:S(2)}) copy-start(pred[21]{0:T(512)(128)(4,1)S(1)} %get-tuple-element.44) | copy-start | bytes 67
  385.8 5.7 %copy-start.17 = (pred[128]{0:T(512)(128)(4,1)S(1)}, pred[128]{0:T(512)(128)(4,1)}, u32[]{:S(2)}) copy-start(pred[128]{0:T(512)(128)(4,1)} %get-tuple-element.15) | copy-start | bytes 388
  385.8 5.7 %copy-start.19 = (pred[128]{0:T(512)(128)(4,1)S(1)}, pred[128]{0:T(512)(128)(4,1)}, u32[]{:S(2)}) copy-start(pred[128]{0:T(512)(128)(4,1)} %get-tuple-element.54) | copy-start | bytes 388
  385.9 5.7 %copy-start.21 = (pred[128]{0:T(512)(128)(4,1)S(1)}, pred[128]{0:T(512)(128)(4,1)}, u32[]{:S(2)}) copy-start(pred[128]{0:T(512)(128)(4,1)} %get-tuple-element.56) | copy-start | bytes 388
  385.9 5.7 %copy-start.23 = (pred[128]{0:T(512)(128)(4,1)S(1)}, pred[128]{0:T(512)(128)(4,1)}, u32[]{:S(2)}) copy-start(pred[128]{0:T(512)(128)(4,1)} %get-tuple-element.58) | copy-start | bytes 388
  385.9 5.7 %copy-start.25 = (f32[128]{0:T(128)S(1)}, f32[128]{0:T(128)}, u32[]{:S(2)}) copy-start(f32[128]{0:T(128)} %get-tuple-element.50) | copy-start | bytes 1540
  385.9 5.7 %copy-start.27 = (f32[128]{0:T(128)S(1)}, f32[128]{0:T(128)}, u32[]{:S(2)}) copy-start(f32[128]{0:T(128)} %get-tuple-element.51) | copy-start | bytes 1540
  385.9 5.7 %copy-start.29 = (f32[128]{0:T(128)S(1)}, f32[128]{0:T(128)}, u32[]{:S(2)}) copy-start(f32[128]{0:T(128)} %get-tuple-element.52) | copy-start | bytes 1540
  385.9 5.7 %copy-start.31 = (f32[128]{0:T(128)S(1)}, f32[128]{0:T(128)}, u32[]{:S(2)}) copy-start(f32[128]{0:T(128)} %get-tuple-element.53) | copy-start | bytes 1540
  385.9 5.7 %copy-start.39 = (f32[14]{0:T(128)S(1)}, f32[14]{0:T(128)}, u32[]{:S(2)}) copy-start(f32[14]{0:T(128)} %get-tuple-element.46) | copy-start | bytes 172
  385.9 5.7 %copy-start.40 = (f32[14]{0:T(128)S(1)}, f32[14]{0:T(128)}, u32[]{:S(2)}) copy-start(f32[14]{0:T(128)} %get-tuple-element.47) | copy-start | bytes 172
  435.8 4.3 copy-start.26
  435.8 4.3 copy-start.28
  435.8 4.3 copy-start.30
  455.2 9.6 %collective-permute-start.5 = (f32[14,4,16,128]{3,2,1,0:T(8,128)S(1)}, f32[14,4,16,128]{3,2,1,0:T(8,128)S(1)}, u32[]{:S(2)}, u32[]{:S(2)}) collective-permute-start(f32[14,4,16,128]{3,2,1,0:T(8,128)S(1)} %slice.507), channel_id=1, source_target_pairs={{64,0},{128,64},{192,128},{65,1},{129,65},{193,129},{66,2},{130,66... | collective-permute-start | bytes 1376264 | tf_op jit(solution)/shard_map/ppermute | solution.py:14
  457.1 12.6 %collective-permute-start.6 = (f32[14,8,4,128]{3,2,1,0:T(4,128)S(1)}, f32[14,8,4,128]{3,2,1,0:T(4,128)S(1)}, u32[]{:S(2)}, u32[]{:S(2)}) collective-permute-start(f32[14,8,4,128]{3,2,1,0:T(4,128)S(1)} %get-tuple-element.31), channel_id=1, source_target_pairs={{1,0},{2,1},{3,2},{4,3},{5,4},{6,5},{7,6},{8,7},{9,8},{10,9},{11,1... | collective-permute-start | bytes 688136 | tf_op jit(solution)/shard_map/ppermute | solution.py:32
  460.7 12.2 %collective-permute-start.7 = (f32[14,8,4,128]{3,2,1,0:T(4,128)S(1)}, f32[14,8,4,128]{3,2,1,0:T(4,128)S(1)}, u32[]{:S(2)}, u32[]{:S(2)}) collective-permute-start(f32[14,8,4,128]{3,2,1,0:T(4,128)S(1)} %get-tuple-element.32), channel_id=1, source_target_pairs={{0,1},{1,2},{2,3},{3,4},{4,5},{5,6},{6,7},{7,8},{8,9},{9,10},{10,1... | collective-permute-start | bytes 688136 | tf_op jit(solution)/shard_map/ppermute | solution.py:29
  483.7 9.5 %collective-permute-start.8 = (f32[14,4,16,128]{3,2,1,0:T(8,128)S(1)}, f32[14,4,16,128]{3,2,1,0:T(8,128)S(1)}, u32[]{:S(2)}, u32[]{:S(2)}) collective-permute-start(f32[14,4,16,128]{3,2,1,0:T(8,128)S(1)} %slice.539), channel_id=1, source_target_pairs={{64,0},{128,64},{192,128},{65,1},{129,65},{193,129},{66,2},{130,66... | collective-permute-start | bytes 1376264 | tf_op jit(solution)/shard_map/ppermute | solution.py:14
  485.6 16.8 %collective-permute-start.10 = (f32[14,8,4,128]{3,2,1,0:T(4,128)S(1)}, f32[14,8,4,128]{3,2,1,0:T(4,128)S(1)}, u32[]{:S(2)}, u32[]{:S(2)}) collective-permute-start(f32[14,8,4,128]{3,2,1,0:T(4,128)S(1)} %get-tuple-element.27), channel_id=1, source_target_pairs={{0,1},{1,2},{2,3},{3,4},{4,5},{5,6},{6,7},{7,8},{8,9},{9,10},{10,1... | collective-permute-start | bytes 688136 | tf_op jit(solution)/shard_map/ppermute | solution.py:29
  490.6 16.1 %collective-permute-start.9 = (f32[14,8,4,128]{3,2,1,0:T(4,128)S(1)}, f32[14,8,4,128]{3,2,1,0:T(4,128)S(1)}, u32[]{:S(2)}, u32[]{:S(2)}) collective-permute-start(f32[14,8,4,128]{3,2,1,0:T(4,128)S(1)} %get-tuple-element.26), channel_id=1, source_target_pairs={{1,0},{2,1},{3,2},{4,3},{5,4},{6,5},{7,6},{8,7},{9,8},{10,9},{11,1... | collective-permute-start | bytes 688136 | tf_op jit(solution)/shard_map/ppermute | solution.py:32
  (28 other events, 70.4 us)
where the time goes:
time: 519 us; the launch traced here: 511 us
  blocking collectives  354 us (68%)
  local copies, waits for them, and re-layouts  73.8 us (14%)
  starting transfers between devices  25.9 us (5%)
  waiting for transfers between devices  22.9 us (4%)
  other arithmetic  21.5 us (4%)
  matrix products  11 us (2%)
    psum x1, blocking collectives, recycle(): mean = lax.psum(sums, 'span') / total_z  354 us
    gather x8, local copies, waits for them, and re-layouts, interpolate(): upper = jnp.take(values, index_row + 1, axis=-1)  23.9 us
    gather x8, local copies, waits for them, and re-layouts, interpolate(): lower = jnp.take(values, index_row, axis=-1)  23.6 us
    ppermute x3, starting transfers between devices, padded_2(): lax.ppermute(lax.slice_in_dim(block, 0, width, axis=dim), axis, backward)  12.5 us
    ppermute x3, waiting for transfers between devices, padded_2(): lax.ppermute(lax.slice_in_dim(block, block.shape[dim] - width, None, axis...  12.4 us
  transfers between devices with their start and end apart: 11, of which 5 were waited for; matrix products, arithmetic and copies ran while one was open for 15% of the time, Pallas kernels for 0%

commit v1 on v0

v1 whole, which is shorter than its diff:
```python
import functools

import jax
import jax.numpy as jnp
from jax import lax
from jax.experimental import pallas as pl
from jax.experimental.pallas import tpu as pltpu
from jax.sharding import PartitionSpec as P

MESH = pl.DeviceIdType.MESH
STENCIL = (0.8, -0.2, 4.0 / 105.0, -1.0 / 280.0)
TIMESTEP = 0.2
VISCOSITY = 0.1
SPECIES, FIELDS, REACT = 9, 14, 21
NY, ROWS, PLANES, HALF = 128, 16, 8, 4
TOP = 8
NZ_CHIPS, NY_CHIPS = 8, 4
YX_PEERS = [(dy, dx) for dy in range(4) for dx in range(2) if (dy, dx) != (0, 0)]
BLENDS = ((0.0, 1.0), (0.75, 0.25), (1.0 / 3.0, 2.0 / 3.0))


def own(h):
    return pl.ds(h * HALF, HALF)


def kernel(
    species_ref, flow_ref, index_ref, frac_ref, mean_gain, fluct_gain, table, rate_const, activation, heat,
    species_out, flow_out,
    x0, x1, x2, out_buf, follow, recycled, ghost, source, picked, weights, basis,
    sums, sums_in, part, part_in, mean_own, mean_in,
    load_sem, store_sem, z_send, z_recv, z0_send, z0_recv, f_send, f_recv, f0_send, f0_recv, r_send, r_recv,
    s_send, s_recv, p_send, p_recv, m_send, m_recv,
):
    stream, span = lax.axis_index("stream"), lax.axis_index("span")
    z, y, xh = span // 8, (span // 2) % 4, span % 2
    right, left = (stream, (span + 1) % 64), (stream, (span + 63) % 64)
    nxt, prev = ((stream + 1) % 4, span), ((stream + 3) % 4, span)
    first, last = stream == 0, stream == 3

    def along_z(group, d):
        return (group, ((z + d) % 8) * 8 + y * 2 + xh)

    def yx_peer(dy, dx):
        return (stream, z * 8 + ((y + dy) % 4) * 2 + (xh + dx) % 2)

    barrier = pltpu.get_barrier_semaphore()

    def hello(device):
        pl.semaphore_signal(barrier, inc=1, device_id=device, device_id_type=MESH)

    hello(left)
    hello(right)
    for d in range(8):
        hello(along_z((stream + 3) % 4, d))
    for d in range(1, 8):
        hello(along_z(stream, d))
    for dy, dx in YX_PEERS:
        hello(yx_peer(dy, dx))

    @pl.when(jnp.logical_not(last))
    def _():
        hello(nxt)

    loads = [
        pltpu.make_async_copy(species_ref, x0.at[pl.ds(0, SPECIES), :, pl.ds(TOP, ROWS)], load_sem.at[0]),
        pltpu.make_async_copy(flow_ref, x0.at[pl.ds(SPECIES, 5), :, pl.ds(TOP, ROWS)], load_sem.at[1]),
    ]
    for c in loads:
        c.start()

    def weight_row(r, _):
        a, b, p, k = table[r, 0], table[r, 1], table[r, 2], rate_const[r]
        for s in range(SPECIES):
            made = jnp.where(p == s, 2.0 * k, 0.0)
            weights[r, s] = made - jnp.where(a == s, k, 0.0) - jnp.where(b == s, k, 0.0)
        weights[r, SPECIES] = heat[r] * k
        return 0

    lax.fori_loop(0, REACT, weight_row, 0)

    pl.semaphore_wait(barrier, 2 + 8 + 7 + 7 + jnp.where(first, 0, 1))

    def remote(src, dst, send, recv, device):
        return pltpu.make_async_remote_copy(
            src_ref=src, dst_ref=dst, send_sem=send, recv_sem=recv, device_id=device, device_id_type=MESH
        )

    parts = ((species_ref, 0, SPECIES), (flow_ref, SPECIES, 5))

    def z0_copies(h):
        made = []
        for i, (ref, at, n) in enumerate(parts):
            made.append(remote(ref.at[:, own(h), pl.ds(0, 4)], x0.at[pl.ds(at, n), own(h), pl.ds(TOP + ROWS, 4)],
                               z0_send.at[h, i, 0], z0_recv.at[h, i, 0], left))
            made.append(remote(ref.at[:, own(h), pl.ds(ROWS - 4, 4)], x0.at[pl.ds(at, n), own(h), pl.ds(TOP - 4, 4)],
                               z0_send.at[h, i, 1], z0_recv.at[h, i, 1], right))
        return made

    def z_copies(buf, k, h):
        return [
            remote(buf.at[:, own(h), pl.ds(TOP, 4)], buf.at[:, own(h), pl.ds(TOP + ROWS, 4)],
                   z_send.at[k, h, 0], z_recv.at[k, h, 0], left),
            remote(buf.at[:, own(h), pl.ds(TOP + ROWS - 4, 4)], buf.at[:, own(h), pl.ds(TOP - 4, 4)],
                   z_send.at[k, h, 1], z_recv.at[k, h, 1], right),
        ]

    def f0_copies():
        return [
            remote(ref.at[:, own(0)], follow.at[0, pl.ds(at, n)], f0_send.at[i], f0_recv.at[i], prev)
            for i, (ref, at, n) in enumerate(parts)
        ]

    def f_copy(buf, k):
        return remote(buf.at[:, own(0), pl.ds(TOP, ROWS)], follow.at[k + 1], f_send.at[k], f_recv.at[k], prev)

    r_copies = [
        remote(ref.at[:, own(1)], recycled.at[pl.ds(at, n)], r_send.at[i], r_recv.at[i], nxt)
        for i, (ref, at, n) in enumerate(parts)
    ]
    for c in z0_copies(0) + r_copies:
        c.start()

    @pl.when(jnp.logical_not(first))
    def _():
        for c in f0_copies():
            c.start()

    for c in z0_copies(1):
        c.start()

    for c in loads:
        c.wait()

    def sum_rows(o, _):
        for i in range(2):
            for j in range(4):
                cells = x0[2 * o + i, HALF + j, pl.ds(TOP, ROWS), :]
                sums[o, pl.ds(4 * i + j, 1), :] = jnp.sum(cells, axis=0, keepdims=True)
        return 0

    lax.fori_loop(0, 7, sum_rows, 0)
    sums[7] = jnp.zeros((8, NY), jnp.float32)

    s_copies = [
        remote(sums.at[(z + d) % 8], sums_in.at[d - 1], s_send.at[d - 1], s_recv.at[d - 1], along_z(stream, d))
        for d in range(1, 8)
    ]
    for c in s_copies:
        c.start()

    lanes = lax.broadcasted_iota(jnp.int32, (8, NY), 1)
    bottom, top = lanes == 0, lanes == NY - 1

    def chemistry(buf, h):
        def pair(i, _):
            at = h * HALF + 2 * i
            cells = (pl.ds(at, 2), pl.ds(TOP, ROWS), slice(None))
            for s in range(SPECIES):
                picked[s] = buf[(s, *cells)]
            cold = jnp.exp(-buf[(13, *cells)])

            def react(t, acc):
                for u in range(3):
                    r = 3 * t + u
                    rate = jnp.exp(-activation[r] * cold) * picked[table[r, 0]] * picked[table[r, 1]]
                    acc = tuple(a + weights[r, s] * rate for s, a in enumerate(acc))
                return acc

            zero = jnp.zeros((2, ROWS, NY), jnp.float32)
            acc = lax.fori_loop(0, REACT // 3, react, (zero,) * 10)
            for s in range(SPECIES):
                source[s, pl.ds(at, 2)] = acc[s]
            for s in range(SPECIES, 13):
                source[s, pl.ds(at, 2)] = zero
            source[13, pl.ds(at, 2)] = acc[SPECIES]
            return 0

        lax.fori_loop(0, 2, pair, 0)

    def advance(buf, k, h, target, row0):
        before, after = BLENDS[k]

        def field(f, _):
            for t in range(2):
                at = TOP + 8 * t
                rows = pl.ds(at, 8)
                mine = [buf[f, p, rows, :] for p in range(PLANES)]
                side = [(ghost if h == 0 else follow.at[k])[f, j, pl.ds(8 * t, 8), :] for j in range(4)]
                line = side + mine if h == 0 else mine + side
                for q in range(HALF):
                    p, c = HALF * h + q, line[4 + q]
                    dx, dz = 0.0, 0.0
                    for o in range(1, 5):
                        dx = dx + STENCIL[o - 1] * (line[4 + q + o] - line[4 + q - o])
                        dz = dz + STENCIL[o - 1] * (buf[f, p, pl.ds(at + o, 8), :] - buf[f, p, pl.ds(at - o, 8), :])
                    down = jnp.where(bottom, 0.0, pltpu.roll(c, 1, 1))
                    up = jnp.where(top, c, pltpu.roll(c, NY - 1, 1))
                    slope = (1.0 + buf[9, p, rows, :]) * dx + buf[11, p, rows, :] * dz
                    change = VISCOSITY * (up - 2.0 * c + down) + source[f, p, pl.ds(8 * t, 8), :] - slope
                    value = after * (c + TIMESTEP * change)
                    if before:
                        value = value + before * x0[f, p, rows, :]
                    target[f, p, pl.ds(row0 + 8 * t, 8), :] = value
            return 0

        lax.fori_loop(0, FIELDS, field, 0)

    def repeat_last(buf, k):
        @pl.when(last)
        def _():
            def field(f, _):
                for j in range(4):
                    follow[k, f, j] = buf[f, PLANES - 1, pl.ds(TOP, ROWS), :]
                return 0

            lax.fori_loop(0, FIELDS, field, 0)

    level = lax.broadcasted_iota(jnp.int32, (1, NY), 1).astype(jnp.float32) / (NY - 1.0)
    blend = 0.5 * (1.0 + jnp.tanh(6.0 * (level - 0.5)))
    from_row = lax.broadcasted_iota(jnp.int32, (NY, NY), 0)
    for b, share in enumerate((1.0 - blend, blend)):
        index, frac = index_ref[pl.ds(b, 1), :], frac_ref[pl.ds(b, 1), :]
        lower = jnp.where(from_row == index, (1.0 - frac) * share, 0.0)
        basis[:, pl.ds(b * NY, NY)] = lower + jnp.where(from_row == index + 1, frac * share, 0.0)

    chemistry(x0, 0)

    for c in s_copies:
        c.wait()
    total = sums[z]
    for d in range(7):
        total = total + sums_in[d]
    part[...] = total
    p_copies = [
        remote(part, part_in.at[i], p_send.at[i], p_recv.at[i], yx_peer(dy, dx)) for i, (dy, dx) in enumerate(YX_PEERS)
    ]
    for c in p_copies:
        c.start()

    chemistry(x0, 1)
    repeat_last(x0, 0)

    for c in p_copies:
        c.wait()
    for i in range(7):
        total = total + part_in[i]
    mean_own[...] = total / 1024.0
    m_copies = [
        remote(mean_own, mean_in.at[z], m_send.at[d], m_recv.at[d], along_z((stream + 1) % 4, d)) for d in range(8)
    ]
    for c in m_copies:
        c.start()

    for c in r_copies:
        c.wait()

    def rescale_fluct(f, _):
        cells = recycled[f].reshape(4 * ROWS, NY)
        both = jnp.dot(cells, basis[...], precision=lax.Precision.HIGHEST, preferred_element_type=jnp.float32)
        value = fluct_gain[0, f] * both[:, :NY] + fluct_gain[1, f] * both[:, NY:]
        ghost[f] = value.reshape(4, ROWS, NY)
        return 0

    lax.fori_loop(0, FIELDS, rescale_fluct, 0)

    for c in m_copies:
        c.wait()

    def rescale_mean(o, _):
        both = jnp.dot(mean_in[o], basis[...], precision=lax.Precision.HIGHEST, preferred_element_type=jnp.float32)
        for i in range(2):
            f = 2 * o + i
            gain = [mean_gain[b, f] - fluct_gain[b, f] for b in range(2)]
            for j in range(4):
                row = both[4 * i + j:4 * i + j + 1]
                ghost[f, j] = ghost[f, j] + (gain[0] * row[:, :NY] + gain[1] * row[:, NY:])
        return 0

    lax.fori_loop(0, 7, rescale_mean, 0)

    def receive(copies):
        for c in copies:
            c.wait_recv()

    stores = []
    buffers = (x0, x1, x2)
    for k in range(3):
        buf = buffers[k]
        target, row0 = (buffers[k + 1], TOP) if k < 2 else (out_buf, 0)
        for h in range(2):
            receive(z0_copies(h) if k == 0 else z_copies(buf, k - 1, h))
            if h == 1:

                @pl.when(jnp.logical_not(last))
                def _():
                    receive(f0_copies() if k == 0 else [f_copy(buf, k - 1)])

            advance(buf, k, h, target, row0)
            if k < 2:
                for c in z_copies(target, k, h):
                    c.start()
                if h == 0:

                    @pl.when(jnp.logical_not(first))
                    def _():
                        f_copy(target, k).start()

                chemistry(target, h)
                if h == 1:
                    repeat_last(target, k + 1)
            else:
                for i, (ref, at, n) in enumerate(((species_out, 0, SPECIES), (flow_out, SPECIES, 5))):
                    c = pltpu.make_async_copy(out_buf.at[pl.ds(at, n), own(h)], ref.at[:, own(h)], store_sem.at[h, i])
                    c.start()
                    stores.append(c)

    for h in range(2):
        for c in z0_copies(h) + z_copies(x1, 0, h) + z_copies(x2, 1, h):
            c.wait_send()

    @pl.when(jnp.logical_not(first))
    def _():
        for c in f0_copies() + [f_copy(x1, 0), f_copy(x2, 1)]:
            c.wait_send()

    for c in stores:
        c.wait()


def on_device(species, flow, index, frac, mean_gain, fluct_gain, table, rate_const, activation, heat):
    vmem, smem, hbm = (pl.BlockSpec(memory_space=m) for m in (pltpu.VMEM, pltpu.SMEM, pl.ANY))
    f32, dma = jnp.float32, pltpu.SemaphoreType.DMA
    extended = pltpu.VMEM((FIELDS, PLANES, 2 * TOP + ROWS, NY), f32)
    scratch = [
        extended, extended, extended,
        pltpu.VMEM((FIELDS, PLANES, ROWS, NY), f32),
        pltpu.VMEM((3, FIELDS, HALF, ROWS, NY), f32),
        pltpu.VMEM((FIELDS, HALF, ROWS, NY), f32),
        pltpu.VMEM((FIELDS, HALF, ROWS, NY), f32),
        pltpu.VMEM((FIELDS, PLANES, ROWS, NY), f32),
        pltpu.VMEM((SPECIES, 2, ROWS, NY), f32),
        pltpu.SMEM((REACT, SPECIES + 1), f32),
        pltpu.VMEM((NY, 2 * NY), f32),
        pltpu.VMEM((8, 8, NY), f32),
        pltpu.VMEM((7, 8, NY), f32),
        pltpu.VMEM((8, NY), f32),
        pltpu.VMEM((7, 8, NY), f32),
        pltpu.VMEM((8, NY), f32),
        pltpu.VMEM((8, 8, NY), f32),
        dma((2,)), dma((2, 2)),
        dma((2, 2, 2)), dma((2, 2, 2)), dma((2, 2, 2)), dma((2, 2, 2)),
        dma((2,)), dma((2,)), dma((2,)), dma((2,)), dma((2,)), dma((2,)),
        dma((7,)), dma((7,)), dma((7,)), dma((7,)), dma((8,)), dma((8,)),
    ]
    return pl.pallas_call(
        kernel,
        out_shape=(jax.ShapeDtypeStruct(species.shape, f32), jax.ShapeDtypeStruct(flow.shape, f32)),
        in_specs=[hbm, hbm, vmem, vmem] + [smem] * 6,
        out_specs=(hbm, hbm),
        scratch_shapes=scratch,
        compiler_params=pltpu.CompilerParams(
            collective_id=0, has_side_effects=True, vmem_limit_bytes=40 * 1024 * 1024
        ),
    )(species, flow, index, frac, mean_gain, fluct_gain, table, rate_const, activation, heat)


def solution(mesh):
    split = P(None, "stream", "span", None)
    return jax.shard_map(
        on_device, mesh=mesh, in_specs=(split, split) + (P(),) * 8, out_specs=(split, split), check_vma=False
    )
```

time: 519 us -> 79.4 us (0.15); the launches traced: 511 us -> 79.2 us
  blocking collectives: 354 us -> 0 us
  Pallas kernels: 0 us -> 74.1 us
  local copies, waits for them, and re-layouts: 73.8 us -> 4.41 us
  starting transfers between devices: 25.9 us -> 0 us
  waiting for transfers between devices: 22.9 us -> 0 us
  other arithmetic: 21.5 us -> 0 us
  matrix products: 11 us -> 0 us
    psum x1 -> x0, blocking collectives: 354 us -> none  [recycle(): mean = lax.psum(sums, 'span') / total_z]
    pallas_call x0 -> x1, Pallas kernels: none -> 74.1 us  [on_device(): pl.pallas_call(kernel, out_shape=(jax.ShapeDtypeStruct(species.shape, f32...]
    gather x22 -> x0, local copies, waits for them, and re-layouts: 57.3 us -> none  [the longest x8 23.9 us: interpolate(): upper = jnp.take(values, index_row + 1, axis=-1)]
    ppermute x11 -> x0, starting transfers between devices: 25.9 us -> none  [the longest x3 12.5 us: padded_2(): lax.ppermute(lax.slice_in_dim(block, 0, width, axis=dim), axis, backward)]
    ppermute x11 -> x0, waiting for transfers between devices: 22.9 us -> none  [the longest x3 12.4 us: padded_2(): lax.ppermute(lax.slice_in_dim(block, block.shape[dim] - width, None, axis...]
    dot_general x6 -> x0, matrix products: 11 us -> none  [the longest x3 5.57 us: tendency(): jnp.einsum('r,rxzy->xzy', heat_release, rates, precision=lax.Precision.HI...]
    add x4 -> x0, other arithmetic: 10.9 us -> none  [the longest x1 4.14 us: on_device(): lifted = start + TIMESTEP * tendency(spread(start), ghost, *extra)]
  transfers between devices with their start and end apart: 11 -> 0, of which waited for: 5 -> 0; matrix products, arithmetic and copies ran while one was open for 15% -> 0% of each run, Pallas kernels for 0% -> 0%
where the time goes in v1:
time: 79.4 us; the launch traced here: 79.2 us
  Pallas kernels  74.1 us (93%)
  local copies, waits for them, and re-layouts  4.41 us (6%)
    pallas_call x1, Pallas kernels, on_device(): pl.pallas_call(kernel, out_shape=(jax.ShapeDtypeStruct(species.shape, f32...  74.1 us
    unnamed x21, local copies, waits for them, and re-layouts  4.41 us

profile of v1, /device:TPU:6, one launch (start us, length us, event | category | flops | bytes accessed | tf_op | source)
XLA Modules:
  0.0 79.2 jit_solution(10028558317921152786)
XLA Ops:
  0.6 0.0 copy-start.8
  0.6 0.0 copy-start.7
  0.7 0.0 copy-start.6
  0.7 0.0 copy-start.5
  0.7 0.0 copy-start.4
  0.7 0.0 copy-start.3
  0.7 0.0 copy-start.2
  0.7 0.8 %copy.12.table = s32[21,3]{1,0:T(8,128)S(1)} copy(s32[21,3]{0,1:T(4,128)} %param.16) | data formatting | bytes 504 | tf_op args[6]
  1.5 0.0 copy-done.8
  1.5 0.0 copy-done.7
  1.5 0.0 copy-done.6
  1.5 0.0 copy-done.5
  1.5 0.0 copy-done.4
  1.5 0.0 copy-done.3
  1.6 0.0 copy-done.2
  1.6 0.0 copy-start
  1.6 1.1 %copy-done = f32[9,8,16,128]{3,2,1,0:T(8,128)S(1)} copy-done((f32[9,8,16,128]{3,2,1,0:T(8,128)S(1)}, f32[9,8,16,128]{3,2,1,0:T(8,128)}, u32[]{:S(2)}) %copy-start) | copy-done | bytes 589848
  2.6 0.0 copy-start.1
  2.6 1.0 %copy-done.1 = f32[5,8,16,128]{3,2,1,0:T(8,128)S(1)} copy-done((f32[5,8,16,128]{3,2,1,0:T(8,128)S(1)}, f32[5,8,16,128]{3,2,1,0:T(8,128)}, u32[]{:S(2)}) %copy-start.1) | copy-done | bytes 327704
  3.6 74.1 %shard_map.113 = (f32[9,8,16,128]{3,2,1,0:T(8,128)S(1)}, f32[5,8,16,128]{3,2,1,0:T(8,128)S(1)}) custom-call(f32[9,8,16,128]{3,2,1,0:T(8,128)S(1)} %copy-done, f32[5,8,16,128]{3,2,1,0:T(8,128)S(1)} %copy-done.1, s32[2,128]{1,0:T(2,128)S(1)} %copy-done.2, f32[2,128]{1,0:T(2,128)S(1)} %copy-done.3, f32[2,14]{1,0:T(2,128)S(1)} %copy-done.4, ...), custom_call_target="tpu_custom_call" | custom-call | tf_op jit(solution)/shard_map/pallas_call | solution.py:355
  77.7 0.8 %copy.15 = f32[9,8,16,128]{3,2,1,0:T(8,128)} copy(f32[9,8,16,128]{3,2,1,0:T(8,128)S(1)} %get-tuple-element.4) | data formatting | bytes 1179648
  78.5 0.7 copy.16
Async XLA Ops:
  0.6 0.9 %copy-start.8 = (f32[21]{0:T(128)S(1)}, f32[21]{0:T(128)}, u32[]{:S(2)}) copy-start(f32[21]{0:T(128)} %heat.1) | copy-start | bytes 256
  0.6 0.9 %copy-start.7 = (f32[21]{0:T(128)S(1)}, f32[21]{0:T(128)}, u32[]{:S(2)}) copy-start(f32[21]{0:T(128)} %activation.1) | copy-start | bytes 256
  0.7 0.9 %copy-start.6 = (f32[21]{0:T(128)S(1)}, f32[21]{0:T(128)}, u32[]{:S(2)}) copy-start(f32[21]{0:T(128)} %rate_const.1) | copy-start | bytes 256
  0.7 0.9 %copy-start.5 = (f32[2,14]{1,0:T(2,128)S(1)}, f32[2,14]{1,0:T(2,128)}, u32[]{:S(2)}) copy-start(f32[2,14]{1,0:T(2,128)} %fluct_gain.1) | copy-start | bytes 340
  0.7 0.9 %copy-start.4 = (f32[2,14]{1,0:T(2,128)S(1)}, f32[2,14]{1,0:T(2,128)}, u32[]{:S(2)}) copy-start(f32[2,14]{1,0:T(2,128)} %mean_gain.1) | copy-start | bytes 340
  0.7 0.9 %copy-start.3 = (f32[2,128]{1,0:T(2,128)S(1)}, f32[2,128]{1,0:T(2,128)}, u32[]{:S(2)}) copy-start(f32[2,128]{1,0:T(2,128)} %frac_ref.1) | copy-start | bytes 3076
  0.7 0.9 %copy-start.2 = (s32[2,128]{1,0:T(2,128)S(1)}, s32[2,128]{1,0:T(2,128)}, u32[]{:S(2)}) copy-start(s32[2,128]{1,0:T(2,128)} %index_ref.1) | copy-start | bytes 3076
  1.6 1.1 %copy-start = (f32[9,8,16,128]{3,2,1,0:T(8,128)S(1)}, f32[9,8,16,128]{3,2,1,0:T(8,128)}, u32[]{:S(2)}) copy-start(f32[9,8,16,128]{3,2,1,0:T(8,128)} %species_ref.1) | copy-start | bytes 1769476
  2.6 1.0 %copy-start.1 = (f32[5,8,16,128]{3,2,1,0:T(8,128)S(1)}, f32[5,8,16,128]{3,2,1,0:T(8,128)}, u32[]{:S(2)}) copy-start(f32[5,8,16,128]{3,2,1,0:T(8,128)} %flow_ref.1) | copy-start | bytes 983044

commit v2 on v1

--- a/solution.py
+++ b/solution.py
@@ -26,7 +26,7 @@
 def kernel(
     species_ref, flow_ref, index_ref, frac_ref, mean_gain, fluct_gain, table, rate_const, activation, heat,
     species_out, flow_out,
-    x0, x1, x2, out_buf, follow, recycled, ghost, source, picked, weights, basis,
+    x0, x1, x2, early, out_buf, follow, recycled, ghost, source, picked, weights, basis, pull,
     sums, sums_in, part, part_in, mean_own, mean_in,
     load_sem, store_sem, z_send, z_recv, z0_send, z0_recv, f_send, f_recv, f0_send, f0_recv, r_send, r_recv,
     s_send, s_recv, p_send, p_recv, m_send, m_recv,
@@ -69,7 +69,7 @@
         c.start()
 
     def weight_row(r, _):
-        a, b, p, k = table[r, 0], table[r, 1], table[r, 2], rate_const[r]
+        a, b, p, k = table[0, r], table[1, r], table[2, r], rate_const[r]
         for s in range(SPECIES):
             made = jnp.where(p == s, 2.0 * k, 0.0)
             weights[r, s] = made - jnp.where(a == s, k, 0.0) - jnp.where(b == s, k, 0.0)
@@ -97,6 +97,8 @@
         return made
 
     def z_copies(buf, k, h):
+        if (k, h) == (0, 0):
+            buf = early
         return [
             remote(buf.at[:, own(h), pl.ds(TOP, 4)], buf.at[:, own(h), pl.ds(TOP + ROWS, 4)],
                    z_send.at[k, h, 0], z_recv.at[k, h, 0], left),
@@ -111,6 +113,8 @@
         ]
 
     def f_copy(buf, k):
+        if k == 0:
+            buf = early
         return remote(buf.at[:, own(0), pl.ds(TOP, ROWS)], follow.at[k + 1], f_send.at[k], f_recv.at[k], prev)
 
     r_copies = [
@@ -162,7 +166,7 @@
             def react(t, acc):
                 for u in range(3):
                     r = 3 * t + u
-                    rate = jnp.exp(-activation[r] * cold) * picked[table[r, 0]] * picked[table[r, 1]]
+                    rate = jnp.exp(-activation[r] * cold) * picked[table[0, r]] * picked[table[1, r]]
                     acc = tuple(a + weights[r, s] * rate for s, a in enumerate(acc))
                 return acc
 
@@ -224,6 +228,8 @@
         basis[:, pl.ds(b * NY, NY)] = lower + jnp.where(from_row == index + 1, frac * share, 0.0)
 
     chemistry(x0, 0)
+    chemistry(x0, 1)
+    repeat_last(x0, 0)
 
     for c in s_copies:
         c.wait()
@@ -237,20 +243,6 @@
     for c in p_copies:
         c.start()
 
-    chemistry(x0, 1)
-    repeat_last(x0, 0)
-
-    for c in p_copies:
-        c.wait()
-    for i in range(7):
-        total = total + part_in[i]
-    mean_own[...] = total / 1024.0
-    m_copies = [
-        remote(mean_own, mean_in.at[z], m_send.at[d], m_recv.at[d], along_z((stream + 1) % 4, d)) for d in range(8)
-    ]
-    for c in m_copies:
-        c.start()
-
     for c in r_copies:
         c.wait()
 
@@ -263,20 +255,58 @@
 
     lax.fori_loop(0, FIELDS, rescale_fluct, 0)
 
+    for c in p_copies:
+        c.wait()
+    for i in range(7):
+        total = total + part_in[i]
+    mean_own[...] = total / 1024.0
+    mean_in[0, z] = mean_own[...]
+    m_copies = [
+        remote(mean_own, mean_in.at[1, z], m_send.at[d], m_recv.at[d], along_z((stream + 1) % 4, d)) for d in range(8)
+    ] + [
+        remote(mean_own, mean_in.at[0, z], m_send.at[7 + d], m_recv.at[7 + d], along_z(stream, d)) for d in range(1, 8)
+    ]
     for c in m_copies:
-        c.wait()
+        c.start()
 
     def rescale_mean(o, _):
-        both = jnp.dot(mean_in[o], basis[...], precision=lax.Precision.HIGHEST, preferred_element_type=jnp.float32)
-        for i in range(2):
-            f = 2 * o + i
-            gain = [mean_gain[b, f] - fluct_gain[b, f] for b in range(2)]
-            for j in range(4):
-                row = both[4 * i + j:4 * i + j + 1]
-                ghost[f, j] = ghost[f, j] + (gain[0] * row[:, :NY] + gain[1] * row[:, NY:])
+        for w in range(2):
+            both = jnp.dot(mean_in[w, o], basis[...], precision=lax.Precision.HIGHEST, preferred_element_type=jnp.float32)
+            for i in range(2):
+                f = 2 * o + i
+                gain = [mean_gain[b, f] - fluct_gain[b, f] for b in range(2)]
+                rows = both[4 * i:4 * i + 4]
+                rows = gain[0] * rows[:, :NY] + gain[1] * rows[:, NY:]
+                for q in range(HALF):
+                    pull[w, f, pl.ds(q, 1), :] = sum(STENCIL[u - 1] * rows[4 + q - u:5 + q - u] for u in range(q + 1, 5))
+                if w == 1:
+                    for j in range(4):
+                        ghost[f, j] = ghost[f, j] + rows[j:j + 1]
         return 0
 
-    lax.fori_loop(0, 7, rescale_mean, 0)
+    def correct_early():
+        blocks = [pl.ds(TOP - 4 + 8 * t, 8) for t in range(3)]
+        factor = [[TIMESTEP * (1.0 + x0[9, q, rows, :]) for rows in blocks] for q in range(HALF)]
+
+        def field(f, _):
+            for q in range(HALF):
+                for t, rows in enumerate(blocks):
+                    x1[f, q, rows, :] = early[f, q, rows, :] + factor[q][t] * pull[1, f, pl.ds(q, 1), :]
+            return 0
+
+        lax.fori_loop(0, FIELDS, field, 0)
+
+    def correct_follow():
+        @pl.when(jnp.logical_not(last))
+        def _():
+            factor = [TIMESTEP * (1.0 + follow[0, 9, q]) for q in range(HALF)]
+
+            def field(f, _):
+                for q in range(HALF):
+                    follow[1, f, q] = follow[1, f, q] + factor[q] * pull[0, f, pl.ds(q, 1), :]
+                return 0
+
+            lax.fori_loop(0, FIELDS, field, 0)
 
     def receive(copies):
         for c in copies:
@@ -288,14 +318,24 @@
         buf = buffers[k]
         target, row0 = (buffers[k + 1], TOP) if k < 2 else (out_buf, 0)
         for h in range(2):
+            if (k, h) == (1, 0):
+                for c in m_copies:
+                    c.wait()
+                lax.fori_loop(0, 7, rescale_mean, 0)
             receive(z0_copies(h) if k == 0 else z_copies(buf, k - 1, h))
+            if (k, h) == (1, 0):
+                correct_early()
+                chemistry(x1, 0)
             if h == 1:
 
                 @pl.when(jnp.logical_not(last))
                 def _():
                     receive(f0_copies() if k == 0 else [f_copy(buf, k - 1)])
 
-            advance(buf, k, h, target, row0)
+                if k == 1:
+                    correct_follow()
+
+            advance(buf, k, h, early if (k, h) == (0, 0) else target, row0)
             if k < 2:
                 for c in z_copies(target, k, h):
                     c.start()
@@ -305,7 +345,8 @@
                     def _():
                         f_copy(target, k).start()
 
-                chemistry(target, h)
+                if (k, h) != (0, 0):
+                    chemistry(target, h)
                 if h == 1:
                     repeat_last(target, k + 1)
             else:
@@ -328,11 +369,12 @@
 
 
 def on_device(species, flow, index, frac, mean_gain, fluct_gain, table, rate_const, activation, heat):
-    vmem, smem, hbm = (pl.BlockSpec(memory_space=m) for m in (pltpu.VMEM, pltpu.SMEM, pl.ANY))
+    vmem, smem, hbm, anywhere = (pl.BlockSpec(memory_space=m) for m in (pltpu.VMEM, pltpu.SMEM, pltpu.HBM, pl.ANY))
     f32, dma = jnp.float32, pltpu.SemaphoreType.DMA
     extended = pltpu.VMEM((FIELDS, PLANES, 2 * TOP + ROWS, NY), f32)
     scratch = [
         extended, extended, extended,
+        pltpu.VMEM((FIELDS, HALF, 2 * TOP + ROWS, NY), f32),
         pltpu.VMEM((FIELDS, PLANES, ROWS, NY), f32),
         pltpu.VMEM((3, FIELDS, HALF, ROWS, NY), f32),
         pltpu.VMEM((FIELDS, HALF, ROWS, NY), f32),
@@ -341,27 +383,28 @@
         pltpu.VMEM((SPECIES, 2, ROWS, NY), f32),
         pltpu.SMEM((REACT, SPECIES + 1), f32),
         pltpu.VMEM((NY, 2 * NY), f32),
+        pltpu.VMEM((2, FIELDS, HALF, NY), f32),
         pltpu.VMEM((8, 8, NY), f32),
         pltpu.VMEM((7, 8, NY), f32),
         pltpu.VMEM((8, NY), f32),
         pltpu.VMEM((7, 8, NY), f32),
         pltpu.VMEM((8, NY), f32),
-        pltpu.VMEM((8, 8, NY), f32),
+        pltpu.VMEM((2, 8, 8, NY), f32),
         dma((2,)), dma((2, 2)),
         dma((2, 2, 2)), dma((2, 2, 2)), dma((2, 2, 2)), dma((2, 2, 2)),
         dma((2,)), dma((2,)), dma((2,)), dma((2,)), dma((2,)), dma((2,)),
-        dma((7,)), dma((7,)), dma((7,)), dma((7,)), dma((8,)), dma((8,)),
+        dma((7,)), dma((7,)), dma((7,)), dma((7,)), dma((15,)), dma((15,)),
     ]
     return pl.pallas_call(
         kernel,
         out_shape=(jax.ShapeDtypeStruct(species.shape, f32), jax.ShapeDtypeStruct(flow.shape, f32)),
         in_specs=[hbm, hbm, vmem, vmem] + [smem] * 6,
-        out_specs=(hbm, hbm),
+        out_specs=(anywhere, anywhere),
         scratch_shapes=scratch,
         compiler_params=pltpu.CompilerParams(
-            collective_id=0, has_side_effects=True, vmem_limit_bytes=40 * 1024 * 1024
+            collective_id=0, has_side_effects=True, vmem_limit_bytes=60 * 1024 * 1024
         ),
-    )(species, flow, index, frac, mean_gain, fluct_gain, table, rate_const, activation, heat)
+    )(species, flow, index, frac, mean_gain, fluct_gain, table.T, rate_const, activation, heat)
 
 
 def solution(mesh):

time: 79.4 us -> 74 us (0.932)
  Pallas kernels: 74.1 us -> 70.4 us
  local copies, waits for them, and re-layouts: 4.41 us -> 2.69 us
    pallas_call x1, Pallas kernels: 74.1 us -> 70.4 us  [on_device(): pl.pallas_call(kernel, out_shape=(jax.ShapeDtypeStruct(species.shape, f32...]
    unnamed x21 -> x4, local copies, waits for them, and re-layouts: 4.41 us -> 2.69 us
where the time goes in v2:
time: 74 us; the launch traced here: 73.8 us
  Pallas kernels  70.4 us (95%)
  local copies, waits for them, and re-layouts  2.69 us (4%)
    pallas_call x1, Pallas kernels, on_device(): pl.pallas_call(kernel, out_shape=(jax.ShapeDtypeStruct(species.shape, f32...  70.4 us
    unnamed x4, local copies, waits for them, and re-layouts  2.69 us

profile of v2, /device:TPU:6, one launch (start us, length us, event | category | flops | bytes accessed | tf_op | source)
XLA Modules:
  0.0 73.8 jit_solution(10504680177004445486)
XLA Ops:
  0.6 70.4 %shard_map.113 = (f32[9,8,16,128]{3,2,1,0:T(8,128)}, f32[5,8,16,128]{3,2,1,0:T(8,128)}) custom-call(f32[9,8,16,128]{3,2,1,0:T(8,128)} %species_ref.1, f32[5,8,16,128]{3,2,1,0:T(8,128)} %flow_ref.1, s32[2,128]{1,0:T(2,128)} %index_ref.1, f32[2,128]{1,0:T(2,128)} %frac_ref.1, f32[2,14]{1,0:T(2,128)} %mean_gain.1, f32[2,14]{1,0:T(2,128)} %fluct_gain.1, ...), custom_call_target="tpu_custom_call" | custom-call | tf_op jit(solution)/shard_map/pallas_call | solution.py:398
  71.1 0.0 copy-start
  71.1 2.0 %copy.14 = f32[9,8,16,128]{3,2,1,0:T(8,128)} copy(f32[9,8,16,128]{3,2,1,0:T(8,128)} %get-tuple-element.4) | data formatting | bytes 1179648
  73.1 0.0 copy-done
  73.1 0.7 copy.15
Async XLA Ops:
  71.1 2.0 %copy-start = (f32[5,8,16,128]{3,2,1,0:T(8,128)S(1)}, f32[5,8,16,128]{3,2,1,0:T(8,128)}, u32[]{:S(2)}) copy-start(f32[5,8,16,128]{3,2,1,0:T(8,128)} %get-tuple-element.5) | copy-start | bytes 983044

commit v3 on v2

--- a/solution.py
+++ b/solution.py
@@ -14,8 +14,6 @@
 SPECIES, FIELDS, REACT = 9, 14, 21
 NY, ROWS, PLANES, HALF = 128, 16, 8, 4
 TOP = 8
-NZ_CHIPS, NY_CHIPS = 8, 4
-YX_PEERS = [(dy, dx) for dy in range(4) for dx in range(2) if (dy, dx) != (0, 0)]
 BLENDS = ((0.0, 1.0), (0.75, 0.25), (1.0 / 3.0, 2.0 / 3.0))
 
 
@@ -26,10 +24,10 @@
 def kernel(
     species_ref, flow_ref, index_ref, frac_ref, mean_gain, fluct_gain, table, rate_const, activation, heat,
     species_out, flow_out,
-    x0, x1, x2, early, out_buf, follow, recycled, ghost, source, picked, weights, basis, pull,
-    sums, sums_in, part, part_in, mean_own, mean_in,
-    load_sem, store_sem, z_send, z_recv, z0_send, z0_recv, f_send, f_recv, f0_send, f0_recv, r_send, r_recv,
-    s_send, s_recv, p_send, p_recv, m_send, m_recv,
+    x0, x1, x2, early, follow, recycled, ghost, source, picked, weights, basis, pull,
+    sums, raw_in, both_sums, sums_in, part, part_in, mean_own, mean_in, bounce,
+    load_sem, z_send, z_recv, z0_send, z0_recv, f_send, f_recv, f0_send, f0_recv, r_send, r_recv,
+    w_send, w_recv, s_send, s_recv, p_send, p_recv, m_send, m_recv, b_send, b_recv, o_send,
 ):
     stream, span = lax.axis_index("stream"), lax.axis_index("span")
     z, y, xh = span // 8, (span // 2) % 4, span % 2
@@ -40,8 +38,11 @@
     def along_z(group, d):
         return (group, ((z + d) % 8) * 8 + y * 2 + xh)
 
-    def yx_peer(dy, dx):
-        return (stream, z * 8 + ((y + dy) % 4) * 2 + (xh + dx) % 2)
+    def along_y(d):
+        return (stream, z * 8 + ((y + d) % 4) * 2 + xh)
+
+    def flip(group, at):
+        return (group, at + 1 - 2 * (at % 2))
 
     barrier = pltpu.get_barrier_semaphore()
 
@@ -50,12 +51,13 @@
 
     hello(left)
     hello(right)
-    for d in range(8):
-        hello(along_z((stream + 3) % 4, d))
+    hello(prev)
+    hello(flip(prev[0], span))
+    hello(flip(stream, span))
     for d in range(1, 8):
         hello(along_z(stream, d))
-    for dy, dx in YX_PEERS:
-        hello(yx_peer(dy, dx))
+    for d in range(1, 4):
+        hello(along_y(d))
 
     @pl.when(jnp.logical_not(last))
     def _():
@@ -78,7 +80,20 @@
 
     lax.fori_loop(0, REACT, weight_row, 0)
 
-    pl.semaphore_wait(barrier, 2 + 8 + 7 + 7 + jnp.where(first, 0, 1))
+    for c in loads:
+        c.wait()
+
+    def sum_rows(o, _):
+        for i in range(2):
+            for j in range(4):
+                cells = x0[2 * o + i, HALF + j, pl.ds(TOP, ROWS), :]
+                sums[o, pl.ds(4 * i + j, 1), :] = jnp.sum(cells, axis=0, keepdims=True)
+        return 0
+
+    lax.fori_loop(0, 7, sum_rows, 0)
+    sums[7] = jnp.zeros((8, NY), jnp.float32)
+
+    pl.semaphore_wait(barrier, 2 + 3 + 7 + 3 + jnp.where(first, 0, 1))
 
     def remote(src, dst, send, recv, device):
         return pltpu.make_async_remote_copy(
@@ -88,13 +103,15 @@
     parts = ((species_ref, 0, SPECIES), (flow_ref, SPECIES, 5))
 
     def z0_copies(h):
-        made = []
-        for i, (ref, at, n) in enumerate(parts):
-            made.append(remote(ref.at[:, own(h), pl.ds(0, 4)], x0.at[pl.ds(at, n), own(h), pl.ds(TOP + ROWS, 4)],
-                               z0_send.at[h, i, 0], z0_recv.at[h, i, 0], left))
-            made.append(remote(ref.at[:, own(h), pl.ds(ROWS - 4, 4)], x0.at[pl.ds(at, n), own(h), pl.ds(TOP - 4, 4)],
-                               z0_send.at[h, i, 1], z0_recv.at[h, i, 1], right))
-        return made
+        return [
+            remote(ref.at[:, own(h), pl.ds(0, 4)], x0.at[pl.ds(at, n), own(h), pl.ds(TOP + ROWS, 4)],
+                   z0_send.at[h, i, 0], z0_recv.at[h, i, 0], left)
+            for i, (ref, at, n) in enumerate(parts)
+        ] + [
+            remote(ref.at[:, own(h), pl.ds(ROWS - 4, 4)], x0.at[pl.ds(at, n), own(h), pl.ds(TOP - 4, 4)],
+                   z0_send.at[h, i, 1], z0_recv.at[h, i, 1], right)
+            for i, (ref, at, n) in enumerate(parts)
+        ]
 
     def z_copies(buf, k, h):
         if (k, h) == (0, 0):
@@ -121,36 +138,47 @@
         remote(ref.at[:, own(1)], recycled.at[pl.ds(at, n)], r_send.at[i], r_recv.at[i], nxt)
         for i, (ref, at, n) in enumerate(parts)
     ]
-    for c in z0_copies(0) + r_copies:
-        c.start()
+    relay_copies = [
+        remote(ref.at[:, own(1)], bounce.at[pl.ds(at, n)], b_send.at[i], b_recv.at[i], flip(0, span))
+        for i, (ref, at, n) in enumerate(parts)
+    ]
+    onward_copies = [
+        remote(bounce.at[pl.ds(at, n)], recycled.at[pl.ds(at, n)], o_send.at[i], r_recv.at[i], flip(0, span))
+        for i, (ref, at, n) in enumerate(parts)
+    ]
+    raw_copies = [
+        remote(sums, raw_in.at[i], w_send.at[i], w_recv.at[i], device)
+        for i, device in enumerate((flip(stream, span), nxt, flip(nxt[0], span)))
+    ]
+    for c in raw_copies:
+        c.start()
+
+    def each_recycled(act):
+        @pl.when(last)
+        def _():
+            for c in relay_copies:
+                act(c)
+
+        @pl.when(jnp.logical_not(last))
+        def _():
+            for c in r_copies:
+                act(c)
+
+    def start(c):
+        c.start()
+
+    each_recycled(start)
 
     @pl.when(jnp.logical_not(first))
     def _():
-        for c in f0_copies():
+        for c in z0_copies(0):
             c.start()
 
-    for c in z0_copies(1):
-        c.start()
-
-    for c in loads:
-        c.wait()
-
-    def sum_rows(o, _):
-        for i in range(2):
-            for j in range(4):
-                cells = x0[2 * o + i, HALF + j, pl.ds(TOP, ROWS), :]
-                sums[o, pl.ds(4 * i + j, 1), :] = jnp.sum(cells, axis=0, keepdims=True)
-        return 0
-
-    lax.fori_loop(0, 7, sum_rows, 0)
-    sums[7] = jnp.zeros((8, NY), jnp.float32)
-
-    s_copies = [
-        remote(sums.at[(z + d) % 8], sums_in.at[d - 1], s_send.at[d - 1], s_recv.at[d - 1], along_z(stream, d))
-        for d in range(1, 8)
-    ]
-    for c in s_copies:
-        c.start()
+
+    @pl.when(jnp.logical_not(first))
+    def _():
+        for c in f0_copies() + z0_copies(1):
+            c.start()
 
     lanes = lax.broadcasted_iota(jnp.int32, (8, NY), 1)
     bottom, top = lanes == 0, lanes == NY - 1
@@ -181,7 +209,7 @@
 
         lax.fori_loop(0, 2, pair, 0)
 
-    def advance(buf, k, h, target, row0):
+    def advance(buf, k, h, store, fields=(0, FIELDS)):
         before, after = BLENDS[k]
 
         def field(f, _):
@@ -204,10 +232,10 @@
                     value = after * (c + TIMESTEP * change)
                     if before:
                         value = value + before * x0[f, p, rows, :]
-                    target[f, p, pl.ds(row0 + 8 * t, 8), :] = value
+                    store(f, p, t, value)
             return 0
 
-        lax.fori_loop(0, FIELDS, field, 0)
+        lax.fori_loop(*fields, field, 0)
 
     def repeat_last(buf, k):
         @pl.when(last)
@@ -228,50 +256,65 @@
         basis[:, pl.ds(b * NY, NY)] = lower + jnp.where(from_row == index + 1, frac * share, 0.0)
 
     chemistry(x0, 0)
+    for c in raw_copies:
+        c.wait()
+    both_sums[:, 0] = sums[...] + raw_in[0]
+    both_sums[:, 1] = raw_in[1] + raw_in[2]
+    s_copies = [
+        remote(both_sums.at[(z + d) % 8], sums_in.at[d - 1], s_send.at[d - 1], s_recv.at[d - 1], along_z(stream, d))
+        for d in range(1, 8)
+    ]
+    for c in s_copies:
+        c.start()
+
     chemistry(x0, 1)
     repeat_last(x0, 0)
 
+    @pl.when(first)
+    def _():
+        for a, b in zip(relay_copies, onward_copies):
+            a.wait_recv()
+            b.start()
+        for c in z0_copies(0) + z0_copies(1):
+            c.start()
+
+
     for c in s_copies:
         c.wait()
-    total = sums[z]
+    total = both_sums[z]
     for d in range(7):
         total = total + sums_in[d]
     part[...] = total
-    p_copies = [
-        remote(part, part_in.at[i], p_send.at[i], p_recv.at[i], yx_peer(dy, dx)) for i, (dy, dx) in enumerate(YX_PEERS)
-    ]
+    p_copies = [remote(part, part_in.at[d - 1], p_send.at[d - 1], p_recv.at[d - 1], along_y(d)) for d in range(1, 4)]
     for c in p_copies:
         c.start()
 
     for c in r_copies:
-        c.wait()
-
-    def rescale_fluct(f, _):
-        cells = recycled[f].reshape(4 * ROWS, NY)
+        c.wait_recv()
+
+    for at in range(0, FIELDS, 7):
+        cells = recycled[pl.ds(at, 7)].reshape(7 * 4 * ROWS, NY)
         both = jnp.dot(cells, basis[...], precision=lax.Precision.HIGHEST, preferred_element_type=jnp.float32)
-        value = fluct_gain[0, f] * both[:, :NY] + fluct_gain[1, f] * both[:, NY:]
-        ghost[f] = value.reshape(4, ROWS, NY)
-        return 0
-
-    lax.fori_loop(0, FIELDS, rescale_fluct, 0)
+        for i in range(7):
+            value = both[i * 4 * ROWS:(i + 1) * 4 * ROWS]
+            value = fluct_gain[0, at + i] * value[:, :NY] + fluct_gain[1, at + i] * value[:, NY:]
+            ghost[at + i] = value.reshape(4, ROWS, NY)
 
     for c in p_copies:
         c.wait()
-    for i in range(7):
+    for i in range(3):
         total = total + part_in[i]
     mean_own[...] = total / 1024.0
-    mean_in[0, z] = mean_own[...]
+    mean_in[z] = mean_own[...]
     m_copies = [
-        remote(mean_own, mean_in.at[1, z], m_send.at[d], m_recv.at[d], along_z((stream + 1) % 4, d)) for d in range(8)
-    ] + [
-        remote(mean_own, mean_in.at[0, z], m_send.at[7 + d], m_recv.at[7 + d], along_z(stream, d)) for d in range(1, 8)
+        remote(mean_own, mean_in.at[z], m_send.at[d - 1], m_recv.at[d - 1], along_z(stream, d)) for d in range(1, 8)
     ]
     for c in m_copies:
         c.start()
 
     def rescale_mean(o, _):
         for w in range(2):
-            both = jnp.dot(mean_in[w, o], basis[...], precision=lax.Precision.HIGHEST, preferred_element_type=jnp.float32)
+            both = jnp.dot(mean_in[o, w], basis[...], precision=lax.Precision.HIGHEST, preferred_element_type=jnp.float32)
             for i in range(2):
                 f = 2 * o + i
                 gain = [mean_gain[b, f] - fluct_gain[b, f] for b in range(2)]
@@ -312,11 +355,10 @@
         for c in copies:
             c.wait_recv()
 
-    stores = []
     buffers = (x0, x1, x2)
     for k in range(3):
         buf = buffers[k]
-        target, row0 = (buffers[k + 1], TOP) if k < 2 else (out_buf, 0)
+        target = buffers[k + 1] if k < 2 else None
         for h in range(2):
             if (k, h) == (1, 0):
                 for c in m_copies:
@@ -335,8 +377,13 @@
                 if k == 1:
                     correct_follow()
 
-            advance(buf, k, h, early if (k, h) == (0, 0) else target, row0)
             if k < 2:
+                into = early if (k, h) == (0, 0) else target
+
+                def store(f, p, t, value):
+                    into[f, p, pl.ds(TOP + 8 * t, 8), :] = value
+
+                advance(buf, k, h, store)
                 for c in z_copies(target, k, h):
                     c.start()
                 if h == 0:
@@ -350,32 +397,39 @@
                 if h == 1:
                     repeat_last(target, k + 1)
             else:
-                for i, (ref, at, n) in enumerate(((species_out, 0, SPECIES), (flow_out, SPECIES, 5))):
-                    c = pltpu.make_async_copy(out_buf.at[pl.ds(at, n), own(h)], ref.at[:, own(h)], store_sem.at[h, i])
-                    c.start()
-                    stores.append(c)
+
+                def store_species(f, p, t, value):
+                    species_out[f, p, pl.ds(8 * t, 8), :] = value
+
+                def store_flow(f, p, t, value):
+                    flow_out[f - SPECIES, p, pl.ds(8 * t, 8), :] = value
+
+                advance(buf, k, h, store_species, (0, SPECIES))
+                advance(buf, k, h, store_flow, (SPECIES, FIELDS))
 
     for h in range(2):
         for c in z0_copies(h) + z_copies(x1, 0, h) + z_copies(x2, 1, h):
             c.wait_send()
+    each_recycled(lambda c: c.wait_send())
+
+    @pl.when(first)
+    def _():
+        for c in onward_copies:
+            c.wait_send()
 
     @pl.when(jnp.logical_not(first))
     def _():
         for c in f0_copies() + [f_copy(x1, 0), f_copy(x2, 1)]:
             c.wait_send()
 
-    for c in stores:
-        c.wait()
-
 
 def on_device(species, flow, index, frac, mean_gain, fluct_gain, table, rate_const, activation, heat):
-    vmem, smem, hbm, anywhere = (pl.BlockSpec(memory_space=m) for m in (pltpu.VMEM, pltpu.SMEM, pltpu.HBM, pl.ANY))
+    vmem, smem, hbm = (pl.BlockSpec(memory_space=m) for m in (pltpu.VMEM, pltpu.SMEM, pltpu.HBM))
     f32, dma = jnp.float32, pltpu.SemaphoreType.DMA
     extended = pltpu.VMEM((FIELDS, PLANES, 2 * TOP + ROWS, NY), f32)
     scratch = [
         extended, extended, extended,
         pltpu.VMEM((FIELDS, HALF, 2 * TOP + ROWS, NY), f32),
-        pltpu.VMEM((FIELDS, PLANES, ROWS, NY), f32),
         pltpu.VMEM((3, FIELDS, HALF, ROWS, NY), f32),
         pltpu.VMEM((FIELDS, HALF, ROWS, NY), f32),
         pltpu.VMEM((FIELDS, HALF, ROWS, NY), f32),
@@ -385,21 +439,25 @@
         pltpu.VMEM((NY, 2 * NY), f32),
         pltpu.VMEM((2, FIELDS, HALF, NY), f32),
         pltpu.VMEM((8, 8, NY), f32),
-        pltpu.VMEM((7, 8, NY), f32),
-        pltpu.VMEM((8, NY), f32),
-        pltpu.VMEM((7, 8, NY), f32),
-        pltpu.VMEM((8, NY), f32),
-        pltpu.VMEM((2, 8, 8, NY), f32),
-        dma((2,)), dma((2, 2)),
+        pltpu.VMEM((3, 8, 8, NY), f32),
+        pltpu.VMEM((8, 2, 8, NY), f32),
+        pltpu.VMEM((7, 2, 8, NY), f32),
+        pltpu.VMEM((2, 8, NY), f32),
+        pltpu.VMEM((3, 2, 8, NY), f32),
+        pltpu.VMEM((2, 8, NY), f32),
+        pltpu.VMEM((8, 2, 8, NY), f32),
+        pltpu.VMEM((FIELDS, HALF, ROWS, NY), f32),
+        dma((2,)),
         dma((2, 2, 2)), dma((2, 2, 2)), dma((2, 2, 2)), dma((2, 2, 2)),
         dma((2,)), dma((2,)), dma((2,)), dma((2,)), dma((2,)), dma((2,)),
-        dma((7,)), dma((7,)), dma((7,)), dma((7,)), dma((15,)), dma((15,)),
+        dma((3,)), dma((3,)), dma((7,)), dma((7,)), dma((3,)), dma((3,)), dma((7,)), dma((7,)),
+        dma((2,)), dma((2,)), dma((2,)),
     ]
     return pl.pallas_call(
         kernel,
-        out_shape=(jax.ShapeDtypeStruct(species.shape, f32), jax.ShapeDtypeStruct(flow.shape, f32)),
+        out_shape=(pltpu.VMEM(species.shape, f32), pltpu.VMEM(flow.shape, f32)),
         in_specs=[hbm, hbm, vmem, vmem] + [smem] * 6,
-        out_specs=(anywhere, anywhere),
+        out_specs=(vmem, vmem),
         scratch_shapes=scratch,
         compiler_params=pltpu.CompilerParams(
             collective_id=0, has_side_effects=True, vmem_limit_bytes=60 * 1024 * 1024

time: 74 us -> 63 us (0.85)
  Pallas kernels: 70.4 us -> 60.7 us
  local copies, waits for them, and re-layouts: 2.69 us -> 1.54 us
    pallas_call x1, Pallas kernels: 70.4 us -> 60.7 us  [on_device(): pl.pallas_call(kernel, out_shape=(pltpu.VMEM(species.shape, f32), pltpu.V...]
    unnamed x4 -> x2, local copies, waits for them, and re-layouts: 2.69 us -> 1.54 us
where the time goes in v3:
time: 63 us; the launch traced here: 62.9 us
  Pallas kernels  60.7 us (96%)
  local copies, waits for them, and re-layouts  1.54 us (2%)
  between operations  0.64 us (1%)
    pallas_call x1, Pallas kernels, on_device(): pl.pallas_call(kernel, out_shape=(pltpu.VMEM(species.shape, f32), pltpu.V...  60.7 us
    unnamed x2, local copies, waits for them, and re-layouts  1.54 us

profile of v3, /device:TPU:6, one launch (start us, length us, event | category | flops | bytes accessed | tf_op | source)
XLA Modules:
  0.0 62.9 jit_solution(1148030829310605108)
XLA Ops:
  0.6 60.7 %shard_map.113 = (f32[9,8,16,128]{3,2,1,0:T(8,128)S(1)}, f32[5,8,16,128]{3,2,1,0:T(8,128)S(1)}) custom-call(f32[9,8,16,128]{3,2,1,0:T(8,128)} %species_ref.1, f32[5,8,16,128]{3,2,1,0:T(8,128)} %flow_ref.1, s32[2,128]{1,0:T(2,128)} %index_ref.1, f32[2,128]{1,0:T(2,128)} %frac_ref.1, f32[2,14]{1,0:T(2,128)} %mean_gain.1, f32[2,14]{1,0:T(2,128)} %fluct_gain.1, ...), custom_call_target="tpu_custom_call" | custom-call | tf_op jit(solution)/shard_map/pallas_call | solution.py:456
  61.3 0.8 %copy.14 = f32[9,8,16,128]{3,2,1,0:T(8,128)} copy(f32[9,8,16,128]{3,2,1,0:T(8,128)S(1)} %get-tuple-element.2) | data formatting | bytes 1179648
  62.1 0.7 %copy.15 = f32[5,8,16,128]{3,2,1,0:T(8,128)} copy(f32[5,8,16,128]{3,2,1,0:T(8,128)S(1)} %get-tuple-element.3) | data formatting | bytes 655360

commit v4 on v3

--- a/solution.py
+++ b/solution.py
@@ -13,6 +13,7 @@
 VISCOSITY = 0.1
 SPECIES, FIELDS, REACT = 9, 14, 21
 NY, ROWS, PLANES, HALF = 128, 16, 8, 4
+GATHER_Z, GATHER_Y = 5, 2
 TOP = 8
 BLENDS = ((0.0, 1.0), (0.75, 0.25), (1.0 / 3.0, 2.0 / 3.0))
 
@@ -27,7 +28,7 @@
     x0, x1, x2, early, follow, recycled, ghost, source, picked, weights, basis, pull,
     sums, raw_in, both_sums, sums_in, part, part_in, mean_own, mean_in, bounce,
     load_sem, z_send, z_recv, z0_send, z0_recv, f_send, f_recv, f0_send, f0_recv, r_send, r_recv,
-    w_send, w_recv, s_send, s_recv, p_send, p_recv, m_send, m_recv, b_send, b_recv, o_send,
+    w_send, w_recv, s_send, s_recv, p_send, p_recv, m_send, m_recv, b_send, b_recv, o_send, all_here,
 ):
     stream, span = lax.axis_index("stream"), lax.axis_index("span")
     z, y, xh = span // 8, (span // 2) % 4, span % 2
@@ -44,6 +45,9 @@
     def flip(group, at):
         return (group, at + 1 - 2 * (at % 2))
 
+    gatherer = (stream, GATHER_Z * 8 + GATHER_Y * 2 + xh)
+    gathers = span == gatherer[1]
+
     barrier = pltpu.get_barrier_semaphore()
 
     def hello(device):
@@ -54,10 +58,10 @@
     hello(prev)
     hello(flip(prev[0], span))
     hello(flip(stream, span))
-    for d in range(1, 8):
-        hello(along_z(stream, d))
-    for d in range(1, 4):
-        hello(along_y(d))
+
+    @pl.when(jnp.logical_not(gathers))
+    def _():
+        hello(gatherer)
 
     @pl.when(jnp.logical_not(last))
     def _():
@@ -93,7 +97,7 @@
     lax.fori_loop(0, 7, sum_rows, 0)
     sums[7] = jnp.zeros((8, NY), jnp.float32)
 
-    pl.semaphore_wait(barrier, 2 + 3 + 7 + 3 + jnp.where(first, 0, 1))
+    pl.semaphore_wait(barrier, 2 + 3 + jnp.where(first, 0, 1) + jnp.where(gathers, 31, 0))
 
     def remote(src, dst, send, recv, device):
         return pltpu.make_async_remote_copy(
@@ -179,6 +183,15 @@
     def _():
         for c in f0_copies() + z0_copies(1):
             c.start()
+
+    @pl.when(gathers)
+    def _():
+        def tell(i, _):
+            device = (stream, ((z + i // 4) % 8) * 8 + ((y + i % 4) % 4) * 2 + xh)
+            pl.semaphore_signal(all_here, inc=1, device_id=device, device_id_type=MESH)
+            return 0
+
+        lax.fori_loop(1, 32, tell, 0)
 
     lanes = lax.broadcasted_iota(jnp.int32, (8, NY), 1)
     bottom, top = lanes == 0, lanes == NY - 1
@@ -255,18 +268,50 @@
         lower = jnp.where(from_row == index, (1.0 - frac) * share, 0.0)
         basis[:, pl.ds(b * NY, NY)] = lower + jnp.where(from_row == index + 1, frac * share, 0.0)
 
-    chemistry(x0, 0)
-    for c in raw_copies:
-        c.wait()
-    both_sums[:, 0] = sums[...] + raw_in[0]
-    both_sums[:, 1] = raw_in[1] + raw_in[2]
     s_copies = [
         remote(both_sums.at[(z + d) % 8], sums_in.at[d - 1], s_send.at[d - 1], s_recv.at[d - 1], along_z(stream, d))
         for d in range(1, 8)
     ]
-    for c in s_copies:
-        c.start()
-
+    p_copies = [remote(part, part_in.at[d - 1], p_send.at[d - 1], p_recv.at[d - 1], along_y(d)) for d in range(1, 4)]
+    m_copies = [
+        remote(mean_own, mean_in.at[z], m_send.at[d - 1], m_recv.at[d - 1], along_z(stream, d)) for d in range(1, 8)
+    ]
+
+    def sums_along_z():
+        for c in raw_copies:
+            c.wait()
+        both_sums[:, 0] = sums[...] + raw_in[0]
+        both_sums[:, 1] = raw_in[1] + raw_in[2]
+
+        @pl.when(jnp.logical_not(gathers))
+        def _():
+            pl.semaphore_wait(all_here, 1)
+
+        for c in s_copies:
+            c.start()
+
+    def sums_along_y():
+        for c in s_copies:
+            c.wait()
+        total = both_sums[z]
+        for d in range(7):
+            total = total + sums_in[d]
+        part[...] = total
+        for c in p_copies:
+            c.start()
+
+    def hand_round():
+        for c in p_copies:
+            c.wait()
+        total = part[...]
+        for i in range(3):
+            total = total + part_in[i]
+        mean_own[...] = total / 1024.0
+        mean_in[z] = mean_own[...]
+        for c in m_copies:
+            c.start()
+
+    chemistry(x0, 0)
     chemistry(x0, 1)
     repeat_last(x0, 0)
 
@@ -278,16 +323,7 @@
         for c in z0_copies(0) + z0_copies(1):
             c.start()
 
-
-    for c in s_copies:
-        c.wait()
-    total = both_sums[z]
-    for d in range(7):
-        total = total + sums_in[d]
-    part[...] = total
-    p_copies = [remote(part, part_in.at[d - 1], p_send.at[d - 1], p_recv.at[d - 1], along_y(d)) for d in range(1, 4)]
-    for c in p_copies:
-        c.start()
+    sums_along_z()
 
     for c in r_copies:
         c.wait_recv()
@@ -299,18 +335,6 @@
             value = both[i * 4 * ROWS:(i + 1) * 4 * ROWS]
             value = fluct_gain[0, at + i] * value[:, :NY] + fluct_gain[1, at + i] * value[:, NY:]
             ghost[at + i] = value.reshape(4, ROWS, NY)
-
-    for c in p_copies:
-        c.wait()
-    for i in range(3):
-        total = total + part_in[i]
-    mean_own[...] = total / 1024.0
-    mean_in[z] = mean_own[...]
-    m_copies = [
-        remote(mean_own, mean_in.at[z], m_send.at[d - 1], m_recv.at[d - 1], along_z(stream, d)) for d in range(1, 8)
-    ]
-    for c in m_copies:
-        c.start()
 
     def rescale_mean(o, _):
         for w in range(2):
@@ -392,6 +416,9 @@
                     def _():
                         f_copy(target, k).start()
 
+                if (k, h) == (0, 0):
+                    sums_along_y()
+                    hand_round()
                 if (k, h) != (0, 0):
                     chemistry(target, h)
                 if h == 1:
@@ -451,7 +478,7 @@
         dma((2, 2, 2)), dma((2, 2, 2)), dma((2, 2, 2)), dma((2, 2, 2)),
         dma((2,)), dma((2,)), dma((2,)), dma((2,)), dma((2,)), dma((2,)),
         dma((3,)), dma((3,)), dma((7,)), dma((7,)), dma((3,)), dma((3,)), dma((7,)), dma((7,)),
-        dma((2,)), dma((2,)), dma((2,)),
+        dma((2,)), dma((2,)), dma((2,)), pltpu.SemaphoreType.REGULAR,
     ]
     return pl.pallas_call(
         kernel,

time: 63 us -> 60.7 us (0.963); the launches traced: 62.9 us -> 59.8 us
  Pallas kernels: 60.7 us -> 57.6 us
    pallas_call x1, Pallas kernels: 60.7 us -> 57.6 us  [on_device(): pl.pallas_call(kernel, out_shape=(pltpu.VMEM(species.shape, f32), pltpu.V...]
where the time goes in v4:
time: 60.7 us; the launch traced here: 59.8 us
  Pallas kernels  57.6 us (95%)
  local copies, waits for them, and re-layouts  1.54 us (3%)
  between operations  0.64 us (1%)
    pallas_call x1, Pallas kernels, on_device(): pl.pallas_call(kernel, out_shape=(pltpu.VMEM(species.shape, f32), pltpu.V...  57.6 us
    unnamed x2, local copies, waits for them, and re-layouts  1.54 us

profile of v4, /device:TPU:6, one launch (start us, length us, event | category | flops | bytes accessed | tf_op | source)
XLA Modules:
  0.0 59.8 jit_solution(3152483145384697631)
XLA Ops:
  0.6 57.6 %shard_map.113 = (f32[9,8,16,128]{3,2,1,0:T(8,128)S(1)}, f32[5,8,16,128]{3,2,1,0:T(8,128)S(1)}) custom-call(f32[9,8,16,128]{3,2,1,0:T(8,128)} %species_ref.1, f32[5,8,16,128]{3,2,1,0:T(8,128)} %flow_ref.1, s32[2,128]{1,0:T(2,128)} %index_ref.1, f32[2,128]{1,0:T(2,128)} %frac_ref.1, f32[2,14]{1,0:T(2,128)} %mean_gain.1, f32[2,14]{1,0:T(2,128)} %fluct_gain.1, ...), custom_call_target="tpu_custom_call" | custom-call | tf_op jit(solution)/shard_map/pallas_call | solution.py:483
  58.2 0.8 %copy.14 = f32[9,8,16,128]{3,2,1,0:T(8,128)} copy(f32[9,8,16,128]{3,2,1,0:T(8,128)S(1)} %get-tuple-element.2) | data formatting | bytes 1179648
  59.0 0.7 %copy.15 = f32[5,8,16,128]{3,2,1,0:T(8,128)} copy(f32[5,8,16,128]{3,2,1,0:T(8,128)S(1)} %get-tuple-element.3) | data formatting | bytes 655360

commit v5 on v4

--- a/solution.py
+++ b/solution.py
@@ -13,7 +13,7 @@
 VISCOSITY = 0.1
 SPECIES, FIELDS, REACT = 9, 14, 21
 NY, ROWS, PLANES, HALF = 128, 16, 8, 4
-GATHER_Z, GATHER_Y = 5, 2
+GATHER_Z, GATHER_Y = 7, 2
 TOP = 8
 BLENDS = ((0.0, 1.0), (0.75, 0.25), (1.0 / 3.0, 2.0 / 3.0))
 
@@ -23,11 +23,11 @@
 
 
 def kernel(
-    species_ref, flow_ref, index_ref, frac_ref, mean_gain, fluct_gain, table, rate_const, activation, heat,
-    species_out, flow_out,
+    species_ref, flow_ref, index_hbm, frac_hbm, mean_gain_hbm, fluct_gain_hbm, table_hbm, rate_const_hbm, activation_hbm, heat_hbm,
+    species_out, flow_out, index_ref, frac_ref, mean_gain, fluct_gain, table, rate_const, activation, heat,
     x0, x1, x2, early, follow, recycled, ghost, source, picked, weights, basis, pull,
     sums, raw_in, both_sums, sums_in, part, part_in, mean_own, mean_in, bounce,
-    load_sem, z_send, z_recv, z0_send, z0_recv, f_send, f_recv, f0_send, f0_recv, r_send, r_recv,
+    load_sem, small_sem, z_send, z_recv, z0_send, z0_recv, f_send, f_recv, f0_send, f0_recv, r_send, r_recv,
     w_send, w_recv, s_send, s_recv, p_send, p_recv, m_send, m_recv, b_send, b_recv, o_send, all_here,
 ):
     stream, span = lax.axis_index("stream"), lax.axis_index("span")
@@ -74,28 +74,11 @@
     for c in loads:
         c.start()
 
-    def weight_row(r, _):
-        a, b, p, k = table[0, r], table[1, r], table[2, r], rate_const[r]
-        for s in range(SPECIES):
-            made = jnp.where(p == s, 2.0 * k, 0.0)
-            weights[r, s] = made - jnp.where(a == s, k, 0.0) - jnp.where(b == s, k, 0.0)
-        weights[r, SPECIES] = heat[r] * k
-        return 0
-
-    lax.fori_loop(0, REACT, weight_row, 0)
-
-    for c in loads:
-        c.wait()
-
-    def sum_rows(o, _):
-        for i in range(2):
-            for j in range(4):
-                cells = x0[2 * o + i, HALF + j, pl.ds(TOP, ROWS), :]
-                sums[o, pl.ds(4 * i + j, 1), :] = jnp.sum(cells, axis=0, keepdims=True)
-        return 0
-
-    lax.fori_loop(0, 7, sum_rows, 0)
-    sums[7] = jnp.zeros((8, NY), jnp.float32)
+    small_from = (index_hbm, frac_hbm, mean_gain_hbm, fluct_gain_hbm, table_hbm, rate_const_hbm, activation_hbm, heat_hbm)
+    small_to = (index_ref, frac_ref, mean_gain, fluct_gain, table, rate_const, activation, heat)
+    small = [pltpu.make_async_copy(a, b, small_sem.at[i]) for i, (a, b) in enumerate(zip(small_from, small_to))]
+    for c in small:
+        c.start()
 
     pl.semaphore_wait(barrier, 2 + 3 + jnp.where(first, 0, 1) + jnp.where(gathers, 31, 0))
 
@@ -154,9 +137,6 @@
         remote(sums, raw_in.at[i], w_send.at[i], w_recv.at[i], device)
         for i, device in enumerate((flip(stream, span), nxt, flip(nxt[0], span)))
     ]
-    for c in raw_copies:
-        c.start()
-
     def each_recycled(act):
         @pl.when(last)
         def _():
@@ -171,13 +151,27 @@
     def start(c):
         c.start()
 
+    for c in loads:
+        c.wait()
+
+    def sum_rows(o, _):
+        for i in range(2):
+            for j in range(4):
+                cells = x0[2 * o + i, HALF + j, pl.ds(TOP, ROWS), :]
+                sums[o, pl.ds(4 * i + j, 1), :] = jnp.sum(cells, axis=0, keepdims=True)
+        return 0
+
+    lax.fori_loop(0, 7, sum_rows, 0)
+    sums[7] = jnp.zeros((8, NY), jnp.float32)
+
+    for c in raw_copies:
+        c.start()
     each_recycled(start)
 
     @pl.when(jnp.logical_not(first))
     def _():
         for c in z0_copies(0):
             c.start()
-
 
     @pl.when(jnp.logical_not(first))
     def _():
@@ -260,6 +254,19 @@
 
             lax.fori_loop(0, FIELDS, field, 0)
 
+    for c in small:
+        c.wait()
+
+    def weight_row(r, _):
+        a, b, p, k = table[0, r], table[1, r], table[2, r], rate_const[r]
+        for s in range(SPECIES):
+            made = jnp.where(p == s, 2.0 * k, 0.0)
+            weights[r, s] = made - jnp.where(a == s, k, 0.0) - jnp.where(b == s, k, 0.0)
+        weights[r, SPECIES] = heat[r] * k
+        return 0
+
+    lax.fori_loop(0, REACT, weight_row, 0)
+
     level = lax.broadcasted_iota(jnp.int32, (1, NY), 1).astype(jnp.float32) / (NY - 1.0)
     blend = 0.5 * (1.0 + jnp.tanh(6.0 * (level - 0.5)))
     from_row = lax.broadcasted_iota(jnp.int32, (NY, NY), 0)
@@ -335,6 +342,10 @@
             value = both[i * 4 * ROWS:(i + 1) * 4 * ROWS]
             value = fluct_gain[0, at + i] * value[:, :NY] + fluct_gain[1, at + i] * value[:, NY:]
             ghost[at + i] = value.reshape(4, ROWS, NY)
+
+    @pl.when(first)
+    def _():
+        sums_along_y()
 
     def rescale_mean(o, _):
         for w in range(2):
@@ -417,7 +428,11 @@
                         f_copy(target, k).start()
 
                 if (k, h) == (0, 0):
-                    sums_along_y()
+
+                    @pl.when(jnp.logical_not(first))
+                    def _():
+                        sums_along_y()
+
                     hand_round()
                 if (k, h) != (0, 0):
                     chemistry(target, h)
@@ -450,11 +465,25 @@
             c.wait_send()
 
 
+def hand_out(species, flow, species_out, flow_out, sem):
+    copies = [
+        pltpu.make_async_copy(a.at[:, own(h)], b.at[:, own(h)], sem.at[i, h])
+        for i, (a, b) in enumerate(((species, species_out), (flow, flow_out)))
+        for h in range(2)
+    ]
+    for c in copies:
+        c.start()
+    for c in copies:
+        c.wait()
+
+
 def on_device(species, flow, index, frac, mean_gain, fluct_gain, table, rate_const, activation, heat):
-    vmem, smem, hbm = (pl.BlockSpec(memory_space=m) for m in (pltpu.VMEM, pltpu.SMEM, pltpu.HBM))
+    vmem, hbm = (pl.BlockSpec(memory_space=m) for m in (pltpu.VMEM, pltpu.HBM))
     f32, dma = jnp.float32, pltpu.SemaphoreType.DMA
     extended = pltpu.VMEM((FIELDS, PLANES, 2 * TOP + ROWS, NY), f32)
-    scratch = [
+    small = (index, frac, mean_gain, fluct_gain, table.T, rate_const, activation, heat)
+    scratch = [(pltpu.VMEM if i < 2 else pltpu.SMEM)(a.shape, a.dtype) for i, a in enumerate(small)]
+    scratch += [
         extended, extended, extended,
         pltpu.VMEM((FIELDS, HALF, 2 * TOP + ROWS, NY), f32),
         pltpu.VMEM((3, FIELDS, HALF, ROWS, NY), f32),
@@ -474,22 +503,29 @@
         pltpu.VMEM((2, 8, NY), f32),
         pltpu.VMEM((8, 2, 8, NY), f32),
         pltpu.VMEM((FIELDS, HALF, ROWS, NY), f32),
-        dma((2,)),
+        dma((2,)), dma((8,)),
         dma((2, 2, 2)), dma((2, 2, 2)), dma((2, 2, 2)), dma((2, 2, 2)),
         dma((2,)), dma((2,)), dma((2,)), dma((2,)), dma((2,)), dma((2,)),
         dma((3,)), dma((3,)), dma((7,)), dma((7,)), dma((3,)), dma((3,)), dma((7,)), dma((7,)),
         dma((2,)), dma((2,)), dma((2,)), pltpu.SemaphoreType.REGULAR,
     ]
-    return pl.pallas_call(
+    results = pl.pallas_call(
         kernel,
         out_shape=(pltpu.VMEM(species.shape, f32), pltpu.VMEM(flow.shape, f32)),
-        in_specs=[hbm, hbm, vmem, vmem] + [smem] * 6,
+        in_specs=[hbm] * 10,
         out_specs=(vmem, vmem),
         scratch_shapes=scratch,
         compiler_params=pltpu.CompilerParams(
             collective_id=0, has_side_effects=True, vmem_limit_bytes=60 * 1024 * 1024
         ),
-    )(species, flow, index, frac, mean_gain, fluct_gain, table.T, rate_const, activation, heat)
+    )(species, flow, *small)
+    return pl.pallas_call(
+        hand_out,
+        out_shape=tuple(jax.ShapeDtypeStruct(a.shape, f32) for a in results),
+        in_specs=[vmem] * 2,
+        out_specs=(hbm, hbm),
+        scratch_shapes=[dma((2, 2))],
+    )(*(pltpu.with_memory_space_constraint(a, pltpu.VMEM) for a in results))
 
 
 def solution(mesh):

time: 60.7 us -> 59 us (0.972)
  local copies, waits for them, and re-layouts: 1.54 us -> 0 us
    unnamed x2 -> x0, local copies, waits for them, and re-layouts: 1.54 us -> none
    pallas_call x0 -> x1, Pallas kernels: none -> 0.95 us  [on_device(): pl.pallas_call(hand_out, out_shape=tuple((jax.ShapeDtypeStruct(a.shape, f...]
    pallas_call x1, Pallas kernels: 57.6 us -> 56.9 us  [on_device(): pl.pallas_call(kernel, out_shape=(pltpu.VMEM(species.shape, f32), pltpu.V...]
where the time goes in v5:
time: 59 us; the launch traced here: 58.5 us
  Pallas kernels  57.8 us (98%)
  between operations  0.64 us (1%)
    pallas_call x1, Pallas kernels, on_device(): pl.pallas_call(kernel, out_shape=(pltpu.VMEM(species.shape, f32), pltpu.V...  56.9 us

profile of v5, /device:TPU:6, one launch (start us, length us, event | category | flops | bytes accessed | tf_op | source)
XLA Modules:
  0.0 58.5 jit_solution(12854320384417005250)
XLA Ops:
  0.6 56.9 %shard_map.113 = (f32[9,8,16,128]{3,2,1,0:T(8,128)S(1)}, f32[5,8,16,128]{3,2,1,0:T(8,128)S(1)}) custom-call(f32[9,8,16,128]{3,2,1,0:T(8,128)} %species_ref.1, f32[5,8,16,128]{3,2,1,0:T(8,128)} %flow_ref.1, s32[2,128]{1,0:T(2,128)} %index_hbm.1, f32[2,128]{1,0:T(2,128)} %frac_hbm.1, f32[2,14]{1,0:T(2,128)} %mean_gain_hbm.1, f32[2,14]{1,0:T(2,128)} %fluct_gain_hbm.1, ...), custom_call_target="tpu_custom_call" | custom-call | tf_op jit(solution)/shard_map/pallas_call | solution.py:512
  57.5 1.0 %shard_map.114 = (f32[9,8,16,128]{3,2,1,0:T(8,128)}, f32[5,8,16,128]{3,2,1,0:T(8,128)}) custom-call(f32[9,8,16,128]{3,2,1,0:T(8,128)S(1)} %get-tuple-element.4.species, f32[5,8,16,128]{3,2,1,0:T(8,128)S(1)} %get-tuple-element.5.flow), custom_call_target="tpu_custom_call" | custom-call | tf_op jit(solution)/shard_map/pallas_call | solution.py:522

commit v6 on v5

--- a/solution.py
+++ b/solution.py
@@ -104,10 +104,10 @@
         if (k, h) == (0, 0):
             buf = early
         return [
+            remote(buf.at[:, own(h), pl.ds(TOP + ROWS - 4, 4)], buf.at[:, own(h), pl.ds(TOP - 4, 4)],
+                   z_send.at[k, h, 1], z_recv.at[k, h, 1], right),
             remote(buf.at[:, own(h), pl.ds(TOP, 4)], buf.at[:, own(h), pl.ds(TOP + ROWS, 4)],
                    z_send.at[k, h, 0], z_recv.at[k, h, 0], left),
-            remote(buf.at[:, own(h), pl.ds(TOP + ROWS - 4, 4)], buf.at[:, own(h), pl.ds(TOP - 4, 4)],
-                   z_send.at[k, h, 1], z_recv.at[k, h, 1], right),
         ]
 
     def f0_copies():
@@ -362,8 +362,7 @@
                         ghost[f, j] = ghost[f, j] + rows[j:j + 1]
         return 0
 
-    def correct_early():
-        blocks = [pl.ds(TOP - 4 + 8 * t, 8) for t in range(3)]
+    def correct_early(blocks):
         factor = [[TIMESTEP * (1.0 + x0[9, q, rows, :]) for rows in blocks] for q in range(HALF)]
 
         def field(f, _):
@@ -399,10 +398,11 @@
                 for c in m_copies:
                     c.wait()
                 lax.fori_loop(0, 7, rescale_mean, 0)
+                correct_early([pl.ds(TOP, 8), pl.ds(TOP + 8, 8)])
+                chemistry(x1, 0)
             receive(z0_copies(h) if k == 0 else z_copies(buf, k - 1, h))
             if (k, h) == (1, 0):
-                correct_early()
-                chemistry(x1, 0)
+                correct_early([pl.ds(TOP - 4, 4), pl.ds(TOP + ROWS, 4)])
             if h == 1:
 
                 @pl.when(jnp.logical_not(last))
@@ -433,7 +433,16 @@
                     def _():
                         sums_along_y()
 
-                    hand_round()
+                    @pl.when(first | (z >= 1))
+                    def _():
+                        hand_round()
+
+                if (k, h) == (0, 1):
+
+                    @pl.when(jnp.logical_not(first | (z >= 1)))
+                    def _():
+                        hand_round()
+
                 if (k, h) != (0, 0):
                     chemistry(target, h)
                 if h == 1:

time: 59 us -> 58.7 us (level)
  no operation moved by 1% of the time
where the time goes in v6:
time: 58.7 us; the launch traced here: 57.9 us
  Pallas kernels  57.3 us (98%)
  between operations  0.64 us (1%)
    pallas_call x1, Pallas kernels, on_device(): pl.pallas_call(kernel, out_shape=(pltpu.VMEM(species.shape, f32), pltpu.V...  56.3 us

profile of v6, /device:TPU:6, one launch (start us, length us, event | category | flops | bytes accessed | tf_op | source)
XLA Modules:
  0.0 57.9 jit_solution(17993848676309400457)
XLA Ops:
  0.6 56.3 %shard_map.113 = (f32[9,8,16,128]{3,2,1,0:T(8,128)S(1)}, f32[5,8,16,128]{3,2,1,0:T(8,128)S(1)}) custom-call(f32[9,8,16,128]{3,2,1,0:T(8,128)} %species_ref.1, f32[5,8,16,128]{3,2,1,0:T(8,128)} %flow_ref.1, s32[2,128]{1,0:T(2,128)} %index_hbm.1, f32[2,128]{1,0:T(2,128)} %frac_hbm.1, f32[2,14]{1,0:T(2,128)} %mean_gain_hbm.1, f32[2,14]{1,0:T(2,128)} %fluct_gain_hbm.1, ...), custom_call_target="tpu_custom_call" | custom-call | tf_op jit(solution)/shard_map/pallas_call | solution.py:521
  57.0 1.0 %shard_map.114 = (f32[9,8,16,128]{3,2,1,0:T(8,128)}, f32[5,8,16,128]{3,2,1,0:T(8,128)}) custom-call(f32[9,8,16,128]{3,2,1,0:T(8,128)S(1)} %get-tuple-element.4.species, f32[5,8,16,128]{3,2,1,0:T(8,128)S(1)} %get-tuple-element.5.flow), custom_call_target="tpu_custom_call" | custom-call | tf_op jit(solution)/shard_map/pallas_call | solution.py:531

commit v7 on v6

--- a/solution.py
+++ b/solution.py
@@ -319,8 +319,6 @@
             c.start()
 
     chemistry(x0, 0)
-    chemistry(x0, 1)
-    repeat_last(x0, 0)
 
     @pl.when(first)
     def _():
@@ -330,6 +328,8 @@
         for c in z0_copies(0) + z0_copies(1):
             c.start()
 
+    chemistry(x0, 1)
+    repeat_last(x0, 0)
     sums_along_z()
 
     for c in r_copies:

time: 58.7 us -> 58 us (0.988); the launches traced: 57.9 us -> 57.9 us
  no operation moved by 1% of the time
where the time goes in v7:
time: 58 us; the launch traced here: 57.9 us
  Pallas kernels  57.3 us (99%)
  between operations  0.64 us (1%)
    pallas_call x1, Pallas kernels, on_device(): pl.pallas_call(kernel, out_shape=(pltpu.VMEM(species.shape, f32), pltpu.V...  56.3 us

profile of v7, /device:TPU:6, one launch (start us, length us, event | category | flops | bytes accessed | tf_op | source)
XLA Modules:
  0.0 57.9 jit_solution(8342226550468820895)
XLA Ops:
  0.6 56.3 %shard_map.113 = (f32[9,8,16,128]{3,2,1,0:T(8,128)S(1)}, f32[5,8,16,128]{3,2,1,0:T(8,128)S(1)}) custom-call(f32[9,8,16,128]{3,2,1,0:T(8,128)} %species_ref.1, f32[5,8,16,128]{3,2,1,0:T(8,128)} %flow_ref.1, s32[2,128]{1,0:T(2,128)} %index_hbm.1, f32[2,128]{1,0:T(2,128)} %frac_hbm.1, f32[2,14]{1,0:T(2,128)} %mean_gain_hbm.1, f32[2,14]{1,0:T(2,128)} %fluct_gain_hbm.1, ...), custom_call_target="tpu_custom_call" | custom-call | tf_op jit(solution)/shard_map/pallas_call | solution.py:521
  57.0 1.0 %shard_map.114 = (f32[9,8,16,128]{3,2,1,0:T(8,128)}, f32[5,8,16,128]{3,2,1,0:T(8,128)}) custom-call(f32[9,8,16,128]{3,2,1,0:T(8,128)S(1)} %get-tuple-element.4.species, f32[5,8,16,128]{3,2,1,0:T(8,128)S(1)} %get-tuple-element.5.flow), custom_call_target="tpu_custom_call" | custom-call | tf_op jit(solution)/shard_map/pallas_call | solution.py:531
